TPU v7x, 32 devices: a whole 2x2x4 slice. The times are simulated.
32 devices in a mesh: groups: 2 (over x), wide: 16 (over z, y, core).
Axes of the slice: x: 2, y: 2, z: 4, core: 2. Of those that a mesh axis runs over, the one named last changes fastest.
Arguments:
- features: bfloat16 [32768, 128], P(('groups', 'wide')), parts along dimension 0, may hold values from -6 to 6
- fetch_ids: int32 [32, 16, 16], P('groups', 'wide'), parts along dimension 0, may hold values from 0 to 1023
- tile_lists: int32 [512, 64], P(('groups', 'wide')), parts along dimension 0, may hold values from 0 to 255
- depth_order: int32 [512, 64], P(('groups', 'wide')), parts along dimension 0, may hold values from 0 to 63, each once within a row
- alpha_codes: int32 [512, 64, 256], P(('groups', 'wide')), parts along dimension 0, may hold values from 0 to 255
- list_counts: int32 [32, 16], P(('groups', 'wide')), parts along dimension 0, may hold values from 1 to 64, 544 in all within a row
- targets: bfloat16 [131072, 1024], P(('groups', 'wide')), parts along dimension 0, may hold values from -6 to 6
- dec_weight: bfloat16 [128, 1024], replicated, may hold values from -0.5 to 0.5
Outputs:
- feat_grad: float32 [32768, 128], P(('groups', 'wide')), parts along dimension 0
- dec_grad: float32 [256, 1024], P(('groups', 'wide')), parts along dimension 0
- loss: float32 [2], P('groups'), parts along dimension 0
There are 2 independent parts, one for each index of `groups`. A program takes and returns all parts, laid end to end along the dimension named above; an argument that names none is the same for every part. Nothing has to cross between parts.
All inputs are finite; a program needn't handle non-finite values.
Results may differ from a plain program's by a relative error of at most 0.0011.
Values may be sent and summed in bfloat16 or wider, within the bound.
No kernel may reach another device: no remote copies, remote signals or barrier semaphores. Data moves between devices by JAX's collectives and lax.ppermute only.
A program may use at most 128 MiB of HBM per device.

v0:
```python
import math

import jax
import jax.numpy as jnp
from jax import lax
from jax.sharding import PartitionSpec as P

ALPHA_TOP = 0.1


def local(
    features, fetch_ids, tile_lists, depth_order, alpha_codes, list_counts, targets, dec_weight
):
    peers = lax.axis_size("wide")
    owned = features.shape[0]
    channels = features.shape[1]
    per_owner = fetch_ids.shape[2]
    requests = fetch_ids[:, 0, :]
    outgoing = features[requests]
    buffer = lax.all_to_all(outgoing, "wide", split_axis=0, concat_axis=0, tiled=True).reshape(
        -1, channels
    )
    tile_count = tile_lists.shape[0]
    pixels_tile = alpha_codes.shape[2]
    slots = jnp.take_along_axis(tile_lists, depth_order, axis=1)
    ordered = jnp.take_along_axis(alpha_codes, depth_order[:, :, None], axis=1)
    positions = jnp.arange(tile_lists.shape[1], dtype=jnp.int32)
    active = (positions[None, :] < list_counts[0][:, None]).astype(jnp.float32)
    alpha = ordered.astype(jnp.float32) * (ALPHA_TOP / 255.0) * active[:, :, None]
    through = jnp.cumprod(1.0 - alpha, axis=1)
    transmit = jnp.concatenate([jnp.ones_like(through[:, :1]), through[:, :-1]], axis=1)
    blend = (transmit * alpha).astype(jnp.bfloat16)
    gathered = buffer[slots]
    composite = jnp.einsum("tkp,tkf->tpf", blend, gathered, preferred_element_type=jnp.float32)
    composite = composite.astype(jnp.bfloat16).reshape(-1, channels)
    decoded = jnp.dot(composite, dec_weight, preferred_element_type=jnp.float32)
    residual = decoded - targets.astype(jnp.float32)
    loss_part = jnp.sum(residual * residual)
    grad_out = residual.astype(jnp.bfloat16)
    grad_comp = lax.dot_general(
        grad_out, dec_weight, (((1,), (1,)), ((), ())), preferred_element_type=jnp.float32
    )
    grad_comp = grad_comp.astype(jnp.bfloat16).reshape(tile_count, pixels_tile, channels)
    grad_slot = jnp.einsum("tkp,tpf->tkf", blend, grad_comp, preferred_element_type=jnp.float32)
    grad_buffer = (
        jnp.zeros(buffer.shape, jnp.float32)
        .at[slots.reshape(-1)]
        .add(grad_slot.reshape(-1, channels))
    )
    returned = lax.all_to_all(
        grad_buffer.reshape(peers, per_owner, channels),
        "wide",
        split_axis=0,
        concat_axis=0,
        tiled=True,
    )
    feat_grad = (
        jnp.zeros((owned, channels), jnp.float32)
        .at[requests.reshape(-1)]
        .add(returned.reshape(-1, channels))
    )
    share = channels // peers
    weight_term = lax.dot_general(
        composite, grad_out, (((0,), (0,)), ((), ())), preferred_element_type=jnp.float32
    )
    weight_total, loss_total = lax.psum((weight_term, loss_part), "wide")
    dec_part = lax.dynamic_slice_in_dim(weight_total, lax.axis_index("wide") * share, share, 0)
    pixel_total = peers * tile_count * pixels_tile
    dec_grad = dec_part * (1.0 / math.sqrt(pixel_total))
    loss = (0.5 * loss_total / (pixel_total * targets.shape[1])).reshape(1)
    return (feat_grad, dec_grad, loss)


def solution(mesh):
    return jax.shard_map(
        local,
        mesh=mesh,
        in_specs=(
            P(("groups", "wide"), None),
            P("groups", "wide", None),
            P(("groups", "wide"), None),
            P(("groups", "wide"), None),
            P(("groups", "wide"), None, None),
            P(("groups", "wide"), None),
            P(("groups", "wide"), None),
            P(),
        ),
        out_specs=(P(("groups", "wide"), None), P(("groups", "wide"), None), P("groups")),
        check_vma=False,
    )
```

profile of v0, /device:TPU:0, one launch (start us, length us, event | category | flops | bytes accessed | tf_op | source)
XLA Modules:
  0.0 172.5 jit_solution(16621778109372514107)
XLA Ops:
  7.2 0.8 compare_select_fusion.2
  8.1 2.3 %gather_fusion = bf16[256,128]{1,0:T(8,128)(2,1)} fusion(bf16[1024,128]{1,0:T(8,128)(2,1)} %param.8, s32[1024]{0:T(1024)S(1)} %pad_clamp_fusion), kind=kCustom, calls=%fused_computation | custom fusion | bytes 132096 | tf_op jit(solution)/shard_map/gather | solution.py:19
  10.4 7.4 %all-to-all-start = ((bf16[16,16,128]{2,1,0:T(8,128)(2,1)}), bf16[16,16,128]{2,1,0:T(8,128)(2,1)S(1)}, u32[]{:S(2)}, u32[]{:S(2)}) async-start(bf16[16,16,128]{2,1,0:T(8,128)(2,1)} %bitcast.6), calls=%async_computation | async-start | bytes 131072 | tf_op jit(solution)/shard_map/all_to_all | solution.py:20
  17.9 0.7 bitcast_or_fusion
  18.6 7.7 %gather_fusion.2 = s32[1024]{0:T(1024)S(1)} fusion(s32[16,64]{1,0:T(8,128)} %param.10, s32[1024]{0:T(1024)S(1)} %reshape.185), kind=kCustom, calls=%fused_computation.2 | custom fusion | bytes 16384 | tf_op jit(solution)/shard_map/jit(take_along_axis)/gather | solution.py:25
  26.5 0.7 compare_select_fusion.1
  27.4 0.7 fusion.17
  28.1 7.3 %gather_fusion.3 = s32[1024,256]{1,0:T(8,128)S(1)} fusion(s32[16,64,256]{2,1,0:T(8,128)S(1)} %copy-done, s32[1024]{0:T(1024)S(1)} %reshape.185), kind=kCustom, calls=%fused_computation.3 | custom fusion | bytes 2105344 | tf_op jit(solution)/shard_map/jit(take_along_axis)/gather | solution.py:26
  35.4 0.7 fusion.3
  36.2 0.8 multiply_convert_fusion
  37.0 3.2 %gather_fusion.1 = bf16[1024,128]{1,0:T(8,128)(2,1)S(1)} fusion(bf16[256,128]{1,0:T(8,128)(2,1)S(1)} %bitcast.26, s32[1024]{0:T(1024)S(1)} %broadcast_clamp_fusion), kind=kCustom, calls=%fused_computation.1 | custom fusion | bytes 528384 | tf_op jit(solution)/shard_map/gather | solution.py:33
  40.2 0.5 convolution_convert_fusion.1
  40.7 7.5 %multiply_reduce_fusion = (f32[]{:T(128)}, f32[4096,1024]{1,0:T(8,128)S(1)}) fusion(bf16[4096,1024]{1,0:T(8,128)(2,1)} %param.14, bf16[4096,128]{1,0:T(8,128)(2,1)S(1)} %bitcast.27, bf16[128,1024]{1,0:T(8,128)(2,1)S(1)} %copy-done.2), kind=kOutput, calls=%fused_computation.6 | convolution fusion | flops 1090519040 | bytes 26476548 | tf_op jit(solution)/shard_map/dot_general | solution.py:36
  48.2 5.7 %copy-done.1 = f32[4096,1024]{1,0:T(8,128)} copy-done((f32[4096,1024]{1,0:T(8,128)}, f32[4096,1024]{1,0:T(8,128)S(1)}, u32[]{:S(2)}) %copy-start.1) | copy-done | bytes 16777240
  53.9 6.5 %fusion.20 = f32[128,1024]{1,0:T(8,128)} fusion(bf16[4096,128]{1,0:T(8,128)(2,1)S(1)} %bitcast.28, f32[4096,1024]{1,0:T(8,128)S(1)} %get-tuple-element.7, bf16[4096,1024]{1,0:T(8,128)(2,1)} %param.14), kind=kOutput, calls=%fused_computation.43 | convolution fusion | flops 1086324736 | bytes 26738688 | tf_op jit(solution)/shard_map/dot_general | solution.py:63
  60.5 10.5 %convolution_convert_fusion = bf16[4096,128]{1,0:T(8,128)(2,1)S(1)} fusion(bf16[128,1024]{1,0:T(8,128)(2,1)S(1)} %copy-done.2, f32[4096,1024]{1,0:T(8,128)} %copy-done.1, bf16[4096,1024]{1,0:T(8,128)(2,1)} %param.14), kind=kOutput, calls=%fused_computation.9 | convolution fusion | flops 1086849024 | bytes 26476544 | tf_op jit(solution)/shard_map/dot_general | solution.py:40
  71.4 6.8 %scatter_custom_fusion = f32[256,128]{1,0:T(8,128)} fusion(s32[1024]{0:T(1024)S(1)} %bitcast.36, f32[1024,128]{1,0:T(8,128)S(1)} %bitcast.33, f32[]{:T(128)} %constant.17.clone.1), kind=kCustom, calls=%fused_computation.26 | custom fusion | flops 131072 | bytes 131076 | tf_op jit(solution)/shard_map/scatter-add | solution.py:48
  78.2 6.0 %all-to-all-start.1 = ((f32[16,16,128]{2,1,0:T(8,128)}), f32[16,16,128]{2,1,0:T(8,128)S(1)}, u32[]{:S(2)}, u32[]{:S(2)}) async-start(f32[16,16,128]{2,1,0:T(8,128)} %bitcast.12), calls=%async_computation.1 | async-start | bytes 262144 | tf_op jit(solution)/shard_map/all_to_all | solution.py:50
  84.2 0.5 broadcast.135
  84.7 0.7 reduce.3
  85.5 34.5 %psum.15 = f32[]{:T(128)} all-reduce(f32[]{:T(128)} %get-tuple-element.6), channel_id=1, replica_groups=mesh['groups'=2,'wide'=16] {'wide'}, use_global_device_ids=true, to_apply=%region_5.6 | all-reduce | flops 1 | bytes 8 | tf_op jit(solution)/shard_map/psum | solution.py:66
  120.7 2.2 %scatter_custom_fusion.1 = f32[1024,128]{1,0:T(8,128)} fusion(s32[256]{0:T(256)S(1)} %bitcast.37, f32[256,128]{1,0:T(8,128)S(1)} %bitcast.34, f32[]{:T(128)} %constant.17.clone.1), kind=kCustom, calls=%fused_computation.24 | custom fusion | flops 32768 | bytes 524292 | tf_op jit(solution)/shard_map/scatter-add | solution.py:60
  122.9 40.3 %all-reduce.3.cloned.1.call-done = f32[128,1024]{1,0:T(8,128)} async-done(((f32[128,1024]{1,0:T(8,128)}), f32[128,1024]{1,0:T(8,128)}) %all-reduce.3.cloned.1.call-update) | async-done | bytes 524304 | tf_op jit(solution)/shard_map/psum | solution.py:66
  163.2 1.4 dynamic-slice_multiply_fusion
  (24 shorter events, 1.1 us)
Async XLA Ops:
  7.2 20.9 %copy-start = (s32[16,64,256]{2,1,0:T(8,128)S(1)}, s32[16,64,256]{2,1,0:T(8,128)}, u32[]{:S(2)}) copy-start(s32[16,64,256]{2,1,0:T(8,128)} %param.12) | copy-start | bytes 3145732
  7.2 33.6 %copy-start.2 = (bf16[128,1024]{1,0:T(8,128)(2,1)S(1)}, bf16[128,1024]{1,0:T(8,128)(2,1)}, u32[]{:S(2)}) copy-start(bf16[128,1024]{1,0:T(8,128)(2,1)} %param.15) | copy-start | bytes 786436
  10.4 26.6 %all-to-all-start = ((bf16[16,16,128]{2,1,0:T(8,128)(2,1)}), bf16[16,16,128]{2,1,0:T(8,128)(2,1)S(1)}, u32[]{:S(2)}, u32[]{:S(2)}) async-start(bf16[16,16,128]{2,1,0:T(8,128)(2,1)} %bitcast.6), calls=%async_computation | async-start | bytes 131072 | tf_op jit(solution)/shard_map/all_to_all | solution.py:20
  17.8 145.4 %all-reduce.3.cloned.1.call-start = ((), (), s32[]{:S(2)}) async-start(), calls=%async_computation.2 | async-start | bytes 1048576 | tf_op jit(solution)/shard_map/psum | solution.py:66
  48.2 5.7 %copy-start.1 = (f32[4096,1024]{1,0:T(8,128)}, f32[4096,1024]{1,0:T(8,128)S(1)}, u32[]{:S(2)}) copy-start(f32[4096,1024]{1,0:T(8,128)S(1)} %get-tuple-element.7) | copy-start | bytes 50331652
  60.5 24.3 %copy-start.3 = (s32[16,1,16]{2,1,0:T(1,128)S(1)}, s32[16,1,16]{2,1,0:T(1,128)}, u32[]{:S(2)}) copy-start(s32[16,1,16]{2,1,0:T(1,128)} %param.9) | copy-start | bytes 3076
  78.2 42.5 %all-to-all-start.1 = ((f32[16,16,128]{2,1,0:T(8,128)}), f32[16,16,128]{2,1,0:T(8,128)S(1)}, u32[]{:S(2)}, u32[]{:S(2)}) async-start(f32[16,16,128]{2,1,0:T(8,128)} %bitcast.12), calls=%async_computation.1 | async-start | bytes 262144 | tf_op jit(solution)/shard_map/all_to_all | solution.py:50
Sparse Core Ops, SparseCore 0:
  71.1 92.0 all-reduce.2
where the time goes:
time: 173 us
  waiting for transfers between devices  40.3 us (23%)
  blocking collectives  34.5 us (20%)
  local copies, waits for them, and re-layouts  27.4 us (16%)
  matrix products  25.4 us (15%)
  between operations  16 us (9%)
  other arithmetic  15.5 us (9%)
  starting transfers between devices  13.4 us (8%)
    psum x1, waiting for transfers between devices, local(): weight_total, loss_total = lax.psum((weight_term, loss_part), 'wide')  40.3 us
    psum x1, blocking collectives, local(): weight_total, loss_total = lax.psum((weight_term, loss_part), 'wide')  34.5 us
    dot_general x1, matrix products, local(): lax.dot_general(grad_out, dec_weight, (((1,), (1,)), ((), ())), preferred...  10.5 us
    gather x3, local copies, waits for them, and re-layouts, local(): slots = jnp.take_along_axis(tile_lists, depth_order, axis=1)  7.88 us
    dot_general x1, matrix products, local(): decoded = jnp.dot(composite, dec_weight, preferred_element_type=jnp.float32)  7.46 us
    all_to_all x1, starting transfers between devices, local(): lax.all_to_all(outgoing, 'wide', split_axis=0, concat_axis=0, tiled=True)  7.39 us
    gather x1, local copies, waits for them, and re-layouts, local(): ordered = jnp.take_along_axis(alpha_codes, depth_order[:, :, None], axis=1)  7.3 us
    scatter-add x1, other arithmetic, local(): grad_buffer = jnp.zeros(buffer.shape, jnp.float32).at[slots.reshape(-1)]....  6.81 us
  transfers between devices with their start and end apart: 3, of which 1 were waited for; matrix products, arithmetic and copies ran while one was open for 17% of the time, Pallas kernels for 0%

commit v1 on v0

v1 whole, which is shorter than its diff:
```python
import functools
import math

import jax
import jax.numpy as jnp
from jax import lax
from jax.experimental import pallas as pl
from jax.experimental.pallas import tpu as pltpu
from jax.sharding import PartitionSpec as P

ALPHA_TOP = 0.1
NN = (((1,), (0,)), ((), ()))
NT = (((1,), (1,)), ((), ()))
TN = (((0,), (0,)), ((), ()))
VMEM = pl.BlockSpec(memory_space=pltpu.VMEM)
SMEM = pl.BlockSpec(memory_space=pltpu.SMEM)
ANY = pl.BlockSpec(memory_space=pl.ANY)


def dot(a, b, dims=NN):
    return lax.dot_general(a, b, dims, preferred_element_type=jnp.float32)


def split(x):
    high = x.astype(jnp.bfloat16)
    return high, (x - high.astype(jnp.float32)).astype(jnp.bfloat16)


def one_hot(condition):
    return jnp.where(condition, 1.0, 0.0).astype(jnp.bfloat16)


def params(mib):
    return pltpu.CompilerParams(vmem_limit_bytes=mib << 20)


def pick_kernel(request_ref, feature_ref, out_ref):
    rows, owned = request_ref.shape[0], feature_ref.shape[0]
    lane = lax.broadcasted_iota(jnp.int32, (rows, owned), 1)
    chosen = one_hot(request_ref[...] == lane)
    out_ref[...] = dot(chosen, feature_ref[...]).astype(jnp.bfloat16)


def blend_pair(order, codes, count_first, count_second, list_len):
    both = 2 * list_len
    row = lax.broadcasted_iota(jnp.int32, (both, both), 0)
    lane = lax.broadcasted_iota(jnp.int32, (both, both), 1)
    same = (row >= list_len) == (lane >= list_len)
    place = order + jnp.where(lane[:1] >= list_len, list_len, 0)
    at = row == place
    rank = jnp.sum(jnp.where(at, lane.astype(jnp.float32), 0.0), axis=1, keepdims=True)
    ahead = same & (lane.astype(jnp.float32) < rank)
    nearer = dot(one_hot(ahead), one_hot(at), NT).astype(jnp.bfloat16)
    alpha = codes.astype(jnp.float32) * (ALPHA_TOP / 255.0)
    high, low = split(jnp.log(1.0 - alpha))
    transmit = jnp.exp(dot(nearer, high) + dot(nearer, low))
    slot = lax.broadcasted_iota(jnp.int32, (both, 1), 0)
    limit = jnp.where(slot < list_len, count_first, count_second + list_len)
    live = rank < limit.astype(jnp.float32)
    return jnp.where(live, transmit * alpha, 0.0).astype(jnp.bfloat16), same


def gram_kernel(
    count_ref,
    list_ref,
    order_ref,
    weight_ref,
    code_hbm,
    target_hbm,
    gram_high_ref,
    gram_low_ref,
    cross_high_ref,
    cross_low_ref,
    back_ref,
    square_high_ref,
    square_low_ref,
    loss_ref,
    codes,
    target,
    hot,
    part_high,
    part_low,
    blends,
    bt_high,
    bt_low,
    code_sem,
    target_sem,
):
    tiles, list_len, pixels = codes.shape
    rows = gram_high_ref.shape[0]
    both = 2 * list_len
    pairs = tiles // 2
    code_copies = [
        pltpu.make_async_copy(
            code_hbm.at[pl.ds(2 * i, 2)], codes.at[pl.ds(2 * i, 2)], code_sem.at[i]
        )
        for i in range(pairs)
    ]
    target_copies = [
        pltpu.make_async_copy(
            target_hbm.at[pl.ds(t * pixels, pixels)],
            target.at[pl.ds(t * pixels, pixels)],
            target_sem.at[t],
        )
        for t in range(tiles)
    ]
    for copy in code_copies + target_copies:
        copy.start()
    weight = weight_ref[...]
    high, low = split(dot(weight, weight, NT))
    square_high_ref[...] = high
    square_low_ref[...] = low
    for i in range(pairs):
        code_copies[i].wait()
        blend, same = blend_pair(
            order_ref[i : i + 1, :],
            codes[2 * i : 2 * i + 2].reshape(both, pixels),
            count_ref[0, 2 * i],
            count_ref[0, 2 * i + 1],
            list_len,
        )
        own = slice(i * both, (i + 1) * both)
        blends[own, :] = blend
        place = lax.broadcasted_iota(jnp.int32, (rows, both), 0)
        chosen = one_hot(list_ref[i : i + 1, :] == place)
        hot[:, own] = chosen
        high, low = split(jnp.where(same, dot(blend, blend, NT), 0.0))
        high, low = split(dot(chosen, high) + dot(chosen, low))
        part_high[:, own] = high
        part_low[:, own] = low
    total = jnp.zeros((8, target.shape[1]), jnp.float32)
    for t in range(tiles):
        target_copies[t].wait()
        goal = target[t * pixels : (t + 1) * pixels, :]
        own = slice(t * list_len, (t + 1) * list_len)
        high, low = split(dot(blends[own, :], goal))
        bt_high[own, :] = high
        bt_low[own, :] = low
        wide = goal.astype(jnp.float32)
        total = total + jnp.sum((wide * wide).reshape(pixels // 8, 8, -1), axis=0)
    loss_ref[...] = jnp.full(loss_ref.shape, jnp.sum(total), jnp.float32)
    chosen = hot[...]
    high, low = split(dot(part_high[...], chosen, NT) + dot(part_low[...], chosen, NT))
    gram_high_ref[...] = high
    gram_low_ref[...] = low
    high, low = split(dot(chosen, bt_high[...]) + dot(chosen, bt_low[...]))
    cross_high_ref[...] = high
    cross_low_ref[...] = low
    back_ref[...] = dot(high, weight, NT) + dot(low, weight, NT)


def gradient_kernel(
    parity_ref,
    buffer_ref,
    gram_high_ref,
    gram_low_ref,
    cross_high_ref,
    cross_low_ref,
    back_ref,
    square_high_ref,
    square_low_ref,
    loss_ref,
    weight_ref,
    send_ref,
    keep_ref,
    grads,
):
    parity = parity_ref[0]
    buffer = buffer_ref[...]
    rows, channels = buffer.shape
    chunks = send_ref.shape[0]
    per_owner = rows // (2 * chunks)
    share = channels // (2 * chunks)
    lanes = 128
    width = weight_ref.shape[1]
    strips = width // lanes
    body = share * strips
    half = channels // 2
    mixed = dot(gram_high_ref[...], buffer) + dot(gram_low_ref[...], buffer)
    high, low = split(mixed)
    square_high = square_high_ref[...]
    back = back_ref[...]
    slope = dot(high, square_high) + dot(low, square_high) + dot(high, square_low_ref[...]) - back
    grads[...] = slope
    loss = loss_ref[...] + jnp.sum(buffer.astype(jnp.float32) * (slope - back))
    source = lax.broadcasted_iota(jnp.int32, (channels, channels), 0)
    goal = lax.broadcasted_iota(jnp.int32, (channels, channels), 1)
    second = goal >= half
    inner = jnp.where(second, goal - half, goal)
    side = jnp.where(second, parity, 1 - parity)
    chunk = inner // share
    wanted = chunk * (2 * share) + side * share + (inner - chunk * share)
    ordered = dot(buffer, one_hot(source == wanted)).astype(jnp.bfloat16)
    core_high, core_low = split(dot(ordered, high, TN) + dot(ordered, low, TN))
    weight = weight_ref[...]
    grad = dot(core_high, weight) + dot(core_low, weight)
    grad = grad - dot(ordered, cross_high_ref[...], TN) - dot(ordered, cross_low_ref[...], TN)
    for number, (ref, which) in enumerate(((send_ref, 1 - parity), (keep_ref, parity))):
        for i in range(chunks):
            top = number * half + i * share
            for j in range(strips):
                ref[i, j * share : (j + 1) * share, :] = grad[
                    top : top + share, j * lanes : (j + 1) * lanes
                ]
            begin = pl.multiple_of((2 * i + which) * per_owner, per_owner)
            ref[i, body : body + per_owner, :] = grads[pl.ds(begin, per_owner), :]
            ref[i, body + per_owner :, :] = loss


def join_kernel(body, per_owner, keep_ref, got_ref, out_ref):
    out_ref[:, :body, :] = keep_ref[:, :body, :] + got_ref[:, :body, :]
    out_ref[:, body : body + per_owner, :] = keep_ref[:, body : body + per_owner, :]
    out_ref[:, body + per_owner : body + 2 * per_owner, :] = got_ref[:, body : body + per_owner, :]
    out_ref[:, body + 2 * per_owner :, :] = (
        keep_ref[:, body + per_owner :, :] + got_ref[:, body + per_owner :, :]
    )


def finish_kernel(
    body, per_owner, dec_scale, loss_scale, request_ref, got_ref, feat_ref, dec_ref, loss_ref
):
    chunks = got_ref.shape[0]
    owned = feat_ref.shape[0]
    share = dec_ref.shape[0]
    lanes = got_ref.shape[2]
    total = jnp.sum(got_ref[:, :body, :], axis=0) * dec_scale
    for j in range(body // share):
        dec_ref[:, j * lanes : (j + 1) * lanes] = total[j * share : (j + 1) * share, :]
    tail = jnp.sum(got_ref[:, body + 2 * per_owner :, :], axis=0)
    loss_ref[...] = tail[:1, :] * loss_scale
    moved = got_ref[:, body : body + 2 * per_owner, :].reshape(chunks * 2 * per_owner, lanes)
    high, low = split(moved)
    place = lax.broadcasted_iota(jnp.int32, (owned, moved.shape[0]), 0)
    chosen = one_hot(place == request_ref[...])
    feat_ref[...] = dot(chosen, high) + dot(chosen, low)


def local(
    features, fetch_ids, tile_lists, depth_order, alpha_codes, list_counts, targets, dec_weight
):
    f32, bf16 = jnp.float32, jnp.bfloat16
    peers = lax.axis_size("wide")
    owned, channels = features.shape
    per_owner = fetch_ids.shape[2]
    rows = peers * per_owner
    tiles, list_len, pixels = alpha_codes.shape
    width = targets.shape[1]
    slots = tiles * list_len
    chunks = peers // 2
    share = channels // peers
    lanes = 128
    body = share * (width // lanes)
    parity = lax.rem(lax.axis_index("wide"), 2)
    requests = fetch_ids[:, 0, :]
    outgoing = pl.pallas_call(
        pick_kernel,
        out_shape=jax.ShapeDtypeStruct((rows, channels), bf16),
        in_specs=[VMEM, VMEM],
        out_specs=VMEM,
        compiler_params=params(32),
        name="pick",
    )(requests.reshape(rows, 1), features)
    buffer = lax.all_to_all(
        outgoing.reshape(peers, per_owner, channels), "wide", split_axis=0, concat_axis=0, tiled=True
    ).reshape(rows, channels)
    shape = jax.ShapeDtypeStruct
    grams = pl.pallas_call(
        gram_kernel,
        out_shape=(
            shape((rows, rows), bf16),
            shape((rows, rows), bf16),
            shape((rows, width), bf16),
            shape((rows, width), bf16),
            shape((rows, channels), f32),
            shape((channels, channels), bf16),
            shape((channels, channels), bf16),
            shape((8, lanes), f32),
        ),
        in_specs=[SMEM, VMEM, VMEM, VMEM, ANY, ANY],
        out_specs=(VMEM,) * 8,
        scratch_shapes=[
            pltpu.VMEM((tiles, list_len, pixels), jnp.int32),
            pltpu.VMEM((tiles * pixels, width), bf16),
            pltpu.VMEM((rows, slots), bf16),
            pltpu.VMEM((rows, slots), bf16),
            pltpu.VMEM((rows, slots), bf16),
            pltpu.VMEM((slots, pixels), bf16),
            pltpu.VMEM((slots, width), bf16),
            pltpu.VMEM((slots, width), bf16),
            pltpu.SemaphoreType.DMA((tiles // 2,)),
            pltpu.SemaphoreType.DMA((tiles,)),
        ],
        cost_estimate=pl.CostEstimate(
            flops=2 * slots * pixels * width + 4 * rows * slots * (width + rows),
            bytes_accessed=targets.size * 2 + alpha_codes.size * 4,
            transcendentals=2 * alpha_codes.size,
        ),
        compiler_params=params(48),
        name="gram",
    )(
        list_counts,
        tile_lists.reshape(tiles // 2, 2 * list_len),
        depth_order.reshape(tiles // 2, 2 * list_len),
        dec_weight,
        alpha_codes,
        targets,
    )
    half_shape = shape((chunks, body + per_owner + 8, lanes), f32)
    send, keep = pl.pallas_call(
        gradient_kernel,
        out_shape=(half_shape, half_shape),
        in_specs=[SMEM] + [VMEM] * 10,
        out_specs=(VMEM, VMEM),
        scratch_shapes=[pltpu.VMEM((rows, channels), f32)],
        compiler_params=params(48),
        name="gradient",
    )(parity.reshape(1), buffer, *grams, dec_weight)
    got = lax.ppermute(send, "wide", [(i, i ^ 1) for i in range(peers)])
    joined = pl.pallas_call(
        functools.partial(join_kernel, body, per_owner),
        out_shape=shape((chunks, body + 2 * per_owner + 8, lanes), f32),
        in_specs=[VMEM, VMEM],
        out_specs=VMEM,
        compiler_params=params(16),
        name="join",
    )(keep, got)
    returned = lax.all_to_all(
        joined,
        "wide",
        split_axis=0,
        concat_axis=0,
        axis_index_groups=[[2 * i + c for i in range(chunks)] for c in range(2)],
        tiled=True,
    )
    sides = requests.reshape(chunks, 2, per_owner)
    sides = jnp.where(parity == 0, sides, sides[:, ::-1]).reshape(1, rows)
    pixel_total = peers * tiles * pixels
    feat_grad, dec_grad, loss = pl.pallas_call(
        functools.partial(
            finish_kernel,
            body,
            per_owner,
            1.0 / math.sqrt(pixel_total),
            0.5 / (pixel_total * width),
        ),
        out_shape=(
            shape((owned, channels), f32),
            shape((share, width), f32),
            shape((1, lanes), f32),
        ),
        in_specs=[VMEM, VMEM],
        out_specs=(VMEM,) * 3,
        compiler_params=params(32),
        name="finish",
    )(sides, returned)
    return (feat_grad, dec_grad, loss[0, :1])


def solution(mesh):
    return jax.shard_map(
        local,
        mesh=mesh,
        in_specs=(
            P(("groups", "wide"), None),
            P("groups", "wide", None),
            P(("groups", "wide"), None),
            P(("groups", "wide"), None),
            P(("groups", "wide"), None, None),
            P(("groups", "wide"), None),
            P(("groups", "wide"), None),
            P(),
        ),
        out_specs=(P(("groups", "wide"), None), P(("groups", "wide"), None), P("groups")),
        check_vma=False,
    )
```

time: 173 us -> 54.2 us (0.31)
  blocking collectives: 34.5 us -> 0 us
  waiting for transfers between devices: 40.3 us -> 13.9 us
  matrix products: 25.4 us -> 0 us
  local copies, waits for them, and re-layouts: 27.4 us -> 6.05 us
  Pallas kernels: 0 us -> 17.9 us
  between operations: 16 us -> 0.72 us
  other arithmetic: 15.5 us -> 1.37 us
    psum x1 -> x0, waiting for transfers between devices: 40.3 us -> none  [local(): weight_total, loss_total = lax.psum((weight_term, loss_part), 'wide')]
    psum x1 -> x0, blocking collectives: 34.5 us -> none  [local(): weight_total, loss_total = lax.psum((weight_term, loss_part), 'wide')]
    dot_general x5 -> x0, matrix products: 25.4 us -> none  [the longest x1 10.5 us: local(): lax.dot_general(grad_out, dec_weight, (((1,), (1,)), ((), ())), preferred...]
    gather x6 -> x0, local copies, waits for them, and re-layouts: 20.7 us -> none  [the longest x3 7.88 us: local(): slots = jnp.take_along_axis(tile_lists, depth_order, axis=1)]
    pallas_call x0 -> x5, Pallas kernels: none -> 17.9 us  [the longest x1 14 us: local(): pl.pallas_call(gram_kernel, out_shape=(shape((rows, rows), bf16), shape((...]
    all_to_all x2, waiting for transfers between devices: 0.01 us -> 12.6 us  [the longest x1 12.6 us: local(): lax.all_to_all(joined, 'wide', split_axis=0, concat_axis=0, axis_index_gr...]
    scatter-add x2 -> x0, other arithmetic: 9.01 us -> none  [the longest x1 6.81 us: local(): grad_buffer = jnp.zeros(buffer.shape, jnp.float32).at[slots.reshape(-1)]....]
    mul x2 -> x0, other arithmetic: 2.04 us -> none  [the longest x1 1.37 us: local(): dec_grad = dec_part * (1.0 / math.sqrt(pixel_total))]
  transfers between devices with their start and end apart: 3 -> 3, of which waited for: 1 -> 2; matrix products, arithmetic and copies ran while one was open for 17% -> 3% of each run, Pallas kernels for 0% -> 26%
where the time goes in v1:
time: 54.2 us; the launch traced here: 53.6 us
  Pallas kernels  17.9 us (33%)
  waiting for transfers between devices  13.9 us (26%)
  starting transfers between devices  13.7 us (25%)
  local copies, waits for them, and re-layouts  6.05 us (11%)
  other arithmetic  1.37 us (3%)
  between operations  0.72 us (1%)
    pallas_call x1, Pallas kernels, local(): pl.pallas_call(gram_kernel, out_shape=(shape((rows, rows), bf16), shape((...  14 us
    all_to_all x1, waiting for transfers between devices, local(): lax.all_to_all(joined, 'wide', split_axis=0, concat_axis=0, axis_index_gr...  12.6 us
    all_to_all x1, starting transfers between devices, local(): lax.all_to_all(outgoing.reshape(peers, per_owner, channels), 'wide', spli...  7.39 us
    all_to_all x1, starting transfers between devices, local(): lax.all_to_all(joined, 'wide', split_axis=0, concat_axis=0, axis_index_gr...  5.87 us
    unnamed x13, local copies, waits for them, and re-layouts  4.3 us
    unnamed x1, other arithmetic  1.37 us
    ppermute x1, waiting for transfers between devices, local(): got = lax.ppermute(send, 'wide', [(i, i ^ 1) for i in range(peers)])  1.3 us
    pallas_call x1, Pallas kernels, local(): pl.pallas_call(functools.partial(finish_kernel, body, per_owner, 1.0 / ma...  1.23 us
  transfers between devices with their start and end apart: 3, of which 2 were waited for; matrix products, arithmetic and copies ran while one was open for 3% of the time, Pallas kernels for 26%

profile of v1, /device:TPU:0, one launch (start us, length us, event | category | flops | bytes accessed | tf_op | source)
XLA Modules:
  0.0 53.6 jit_solution(11236227665242082788)
XLA Ops:
  0.6 0.0 copy-start.1
  0.6 0.5 broadcast.4
  1.2 1.4 %reduce.3 = s32[16,16]{1,0:T(8,128)S(1)} reduce(s32[16,1,16]{2,1,0:T(1,128)} %param.9, s32[]{:T(128)} %broadcast.4), dimensions={1}, to_apply=%param.9.reduce_sub_computation.3 | reduce | bytes 2052 | tf_op args[1]
  2.5 0.1 reshape_squeeze.8.request_ref
  2.6 0.0 copy-start.3
  2.6 0.9 %copy-done.3 = bf16[1024,128]{1,0:T(8,128)(2,1)S(1)} copy-done((bf16[1024,128]{1,0:T(8,128)(2,1)S(1)}, bf16[1024,128]{1,0:T(8,128)(2,1)}, u32[]{:S(2)}) %copy-start.3) | copy-done | bytes 262168
  3.6 1.0 %pick.1 = bf16[256,128]{1,0:T(8,128)(2,1)} custom-call(s32[256,1]{1,0:T(8,128)S(1)} %reshape_squeeze.8.request_ref, bf16[1024,128]{1,0:T(8,128)(2,1)S(1)} %copy-done.3), custom_call_target="tpu_custom_call" | custom-call | tf_op jit(solution)/shard_map/pick/pallas_call | solution.py:255
  4.6 7.4 %all-to-all-start = ((bf16[16,16,128]{2,1,0:T(8,128)(2,1)}), bf16[16,16,128]{2,1,0:T(8,128)(2,1)S(1)}, u32[]{:S(2)}, u32[]{:S(2)}) async-start(bf16[16,16,128]{2,1,0:T(8,128)(2,1)} %bitcast.2), calls=%async_computation | async-start | bytes 131072 | tf_op jit(solution)/shard_map/all_to_all | solution.py:263
  12.0 0.8 %reshape.28.list_ref = s32[8,128]{1,0:T(8,128)S(1)} reshape(s32[16,64]{1,0:T(8,128)} %param.10) | data formatting | bytes 8192 | tf_op jit(solution)/shard_map/reshape | solution.py:302
  12.8 0.8 %reshape.29.order_ref = s32[8,128]{1,0:T(8,128)S(1)} reshape(s32[16,64]{1,0:T(8,128)} %param.11) | data formatting | bytes 8192 | tf_op jit(solution)/shard_map/reshape | solution.py:303
  13.5 0.9 %copy-done = bf16[128,1024]{1,0:T(8,128)(2,1)S(1)} copy-done((bf16[128,1024]{1,0:T(8,128)(2,1)S(1)}, bf16[128,1024]{1,0:T(8,128)(2,1)}, u32[]{:S(2)}) %copy-start) | copy-done | bytes 262168
  14.5 1.2 %copy-done.2 = s32[16,64,256]{2,1,0:T(8,128)S(1)} copy-done((s32[16,64,256]{2,1,0:T(8,128)S(1)}, s32[16,64,256]{2,1,0:T(8,128)}, u32[]{:S(2)}) %copy-start.2) | copy-done | bytes 1048600
  15.7 0.7 %copy-done.4 = s32[1,16]{1,0:T(1,128)S(1)} copy-done((s32[1,16]{1,0:T(1,128)S(1)}, s32[1,16]{1,0:T(1,128)}, u32[]{:S(2)}) %copy-start.4) | copy-done | bytes 88
  16.4 14.0 %gram.1 = (bf16[256,256]{1,0:T(8,128)(2,1)S(1)}, bf16[256,256]{1,0:T(8,128)(2,1)S(1)}, bf16[256,1024]{1,0:T(8,128)(2,1)S(1)}, bf16[256,1024]{1,0:T(8,128)(2,1)S(...) custom-call(s32[1,16]{1,0:T(1,128)S(1)} %copy-done.4, ...), custom_call_target="tpu_custom_call" | custom-call | flops 1879048192 | bytes 9437184 | tf_op jit(solution)/shard_map/gram/pallas_call | solution.py:267
  30.4 0.0 all-to-all-done
  30.4 0.0 copy-done.1
  30.4 0.9 %gradient.1 = (f32[8,88,128]{2,1,0:T(8,128)S(1)}, f32[8,88,128]{2,1,0:T(8,128)S(1)}) custom-call(s32[1]{0:T(128)} %bitcast.1.parity_ref, bf16[256,128]{1,0:T(8,128)(2,1)S(1)} %bitcast.9, bf16[256,256]{1,0:T(8,128)(2,1)S(1)} %get-tuple-element.16.gram_high_ref, bf16[256,256]{1,0:T(8,128)(2,1)S(1)} %get-tuple-element.17.gram_low_ref, ...), custom_call_target="tpu_custom_call" | custom-call | tf_op jit(solution)/shard_map/gradient/pallas_call | solution.py:309
  31.3 0.5 collective-permute-start
  31.7 1.3 %collective-permute-done.got_ref = f32[8,88,128]{2,1,0:T(8,128)S(1)} collective-permute-done((f32[8,88,128]{2,1,0:T(8,128)S(1)}, f32[8,88,128]{2,1,0:T(8,128)S(1)}, u32[]{:S(2)}, u32[]{:S(2)}) %collective-permute-start) | collective-permute-done | bytes 360480 | tf_op jit(solution)/shard_map/ppermute | solution.py:318
  33.0 0.8 %join.1 = f32[8,104,128]{2,1,0:T(8,128)} custom-call(f32[8,88,128]{2,1,0:T(8,128)S(1)} %get-tuple-element.24.keep_ref, f32[8,88,128]{2,1,0:T(8,128)S(1)} %collective-permute-done.got_ref), custom_call_target="tpu_custom_call" | custom-call | tf_op jit(solution)/shard_map/join/pallas_call | solution.py:319
  33.8 5.9 %all-to-all-start.1 = ((f32[8,104,128]{2,1,0:T(8,128)}), f32[8,104,128]{2,1,0:T(8,128)S(1)}, u32[]{:S(2)}, u32[]{:S(2)}) async-start(f32[8,104,128]{2,1,0:T(8,128)} %join.1), calls=%async_computation.1 | async-start | bytes 851968 | tf_op jit(solution)/shard_map/all_to_all | solution.py:327
  39.8 0.1 reshape.24.request_ref
  39.8 12.6 %all-to-all-done.1.got_ref = f32[8,104,128]{2,1,0:T(8,128)S(1)} async-done(((f32[8,104,128]{2,1,0:T(8,128)}), f32[8,104,128]{2,1,0:T(8,128)S(1)}, u32[]{:S(2)}, u32[]{:S(2)}) %all-to-all-start.1) | async-done | bytes 426016 | tf_op jit(solution)/shard_map/all_to_all | solution.py:327
  52.4 1.2 %finish.1 = (f32[1024,128]{1,0:T(8,128)}, f32[8,1024]{1,0:T(8,128)}, f32[1,128]{1,0:T(1,128)}) custom-call(s32[1,256]{1,0:T(1,128)S(1)} %reshape.24.request_ref, f32[8,104,128]{2,1,0:T(8,128)S(1)} %all-to-all-done.1.got_ref), custom_call_target="tpu_custom_call" | custom-call | tf_op jit(solution)/shard_map/finish/pallas_call | solution.py:338
  (7 shorter events, 0.0 us)
Async XLA Ops:
  0.6 29.8 %copy-start.1 = (bf16[128,1024]{1,0:T(8,128)(2,1)S(1)}, bf16[128,1024]{1,0:T(8,128)(2,1)}, u32[]{:S(2)}) copy-start(bf16[128,1024]{1,0:T(8,128)(2,1)} %weight_ref.3) | copy-start | bytes 786436
  2.6 1.0 %copy-start.3 = (bf16[1024,128]{1,0:T(8,128)(2,1)S(1)}, bf16[1024,128]{1,0:T(8,128)(2,1)}, u32[]{:S(2)}) copy-start(bf16[1024,128]{1,0:T(8,128)(2,1)} %feature_ref.1) | copy-start | bytes 786436
  3.6 36.1 %copy-start.5 = (s32[16,1,16]{2,1,0:T(1,128)S(1)}, s32[16,1,16]{2,1,0:T(1,128)}, u32[]{:S(2)}) copy-start(s32[16,1,16]{2,1,0:T(1,128)} %param.9) | copy-start | bytes 3076
  4.6 25.8 %all-to-all-start = ((bf16[16,16,128]{2,1,0:T(8,128)(2,1)}), bf16[16,16,128]{2,1,0:T(8,128)(2,1)S(1)}, u32[]{:S(2)}, u32[]{:S(2)}) async-start(bf16[16,16,128]{2,1,0:T(8,128)(2,1)} %bitcast.2), calls=%async_computation | async-start | bytes 131072 | tf_op jit(solution)/shard_map/all_to_all | solution.py:263
  13.5 0.9 %copy-start = (bf16[128,1024]{1,0:T(8,128)(2,1)S(1)}, bf16[128,1024]{1,0:T(8,128)(2,1)}, u32[]{:S(2)}) copy-start(bf16[128,1024]{1,0:T(8,128)(2,1)} %weight_ref.3) | copy-start | bytes 786436
  14.5 1.2 %copy-start.2 = (s32[16,64,256]{2,1,0:T(8,128)S(1)}, s32[16,64,256]{2,1,0:T(8,128)}, u32[]{:S(2)}) copy-start(s32[16,64,256]{2,1,0:T(8,128)} %code_hbm.1) | copy-start | bytes 3145732
  15.7 0.7 %copy-start.4 = (s32[1,16]{1,0:T(1,128)S(1)}, s32[1,16]{1,0:T(1,128)}, u32[]{:S(2)}) copy-start(s32[1,16]{1,0:T(1,128)} %count_ref.1) | copy-start | bytes 196
  31.3 1.8 %collective-permute-start = (f32[8,88,128]{2,1,0:T(8,128)S(1)}, f32[8,88,128]{2,1,0:T(8,128)S(1)}, u32[]{:S(2)}, u32[]{:S(2)}) collective-permute-start(f32[8,88,128]{2,1,0:T(8,128)S(1)} %get-tuple-element.25), channel_id=1, source_target_pairs={{0,1},{1,0},{2,3},{3,2},{4,5},{5,4},{6,7},{7,6},{8,9},{9,8},{10,11... | collective-permute-start | bytes 1081352 | tf_op jit(solution)/shard_map/ppermute | solution.py:318
  33.8 18.6 %all-to-all-start.1 = ((f32[8,104,128]{2,1,0:T(8,128)}), f32[8,104,128]{2,1,0:T(8,128)S(1)}, u32[]{:S(2)}, u32[]{:S(2)}) async-start(f32[8,104,128]{2,1,0:T(8,128)} %join.1), calls=%async_computation.1 | async-start | bytes 851968 | tf_op jit(solution)/shard_map/all_to_all | solution.py:327

commit v2 on v1

v2 whole, which is shorter than its diff:
```python
import functools
import math

import jax
import jax.numpy as jnp
from jax import lax
from jax.experimental import pallas as pl
from jax.experimental.pallas import tpu as pltpu
from jax.sharding import PartitionSpec as P

ALPHA_TOP = 0.1
NN = (((1,), (0,)), ((), ()))
NT = (((1,), (1,)), ((), ()))
TN = (((0,), (0,)), ((), ()))
VMEM = pl.BlockSpec(memory_space=pltpu.VMEM)
SMEM = pl.BlockSpec(memory_space=pltpu.SMEM)
ANY = pl.BlockSpec(memory_space=pl.ANY)
HBM = pl.BlockSpec(memory_space=pltpu.HBM)
CODE_TOP = 32000.0
LOSS_TOP = 16384.0
META = 16


def dot(a, b, dims=NN):
    return lax.dot_general(a, b, dims, preferred_element_type=jnp.float32)


def split(x):
    high = x.astype(jnp.bfloat16)
    return high, (x - high.astype(jnp.float32)).astype(jnp.bfloat16)


def one_hot(condition):
    return jnp.where(condition, 1.0, 0.0).astype(jnp.bfloat16)


def pin(x):
    return pltpu.with_memory_space_constraint(x, pltpu.HBM)


def params(mib):
    return pltpu.CompilerParams(vmem_limit_bytes=mib << 20)


def pick_kernel(request_ref, feature_hbm, out_ref, held, sem):
    copy = pltpu.make_async_copy(feature_hbm, held, sem)
    copy.start()
    peers, _, per_owner = request_ref.shape
    owned = held.shape[0]
    lane = lax.broadcasted_iota(jnp.int32, (peers, per_owner, owned), 2)
    wanted = request_ref[...][:, 0, :]
    chosen = jnp.where(wanted[:, :, None] == lane, 1.0, 0.0)
    chosen = chosen.reshape(peers * per_owner, owned).astype(jnp.bfloat16)
    copy.wait()
    out_ref[...] = dot(chosen, held[...]).astype(jnp.bfloat16)


def gram_kernel(
    count_hbm,
    list_hbm,
    order_hbm,
    weight_hbm,
    code_hbm,
    target_hbm,
    gram_high_ref,
    gram_low_ref,
    cross_high_ref,
    cross_low_ref,
    back_ref,
    square_high_ref,
    square_low_ref,
    loss_ref,
    counts,
    lists,
    orders,
    weights,
    codes,
    target,
    hot,
    blends,
    bt_high,
    bt_low,
    cross,
    first_sem,
    target_sem,
):
    tiles, list_len, pixels = codes.shape
    rows = gram_high_ref.shape[0]
    both = 2 * list_len
    pairs = tiles // 2
    small = [
        pltpu.make_async_copy(source, goal, first_sem.at[i])
        for i, (source, goal) in enumerate(
            (
                (count_hbm, counts),
                (list_hbm, lists),
                (order_hbm, orders),
                (code_hbm, codes),
                (weight_hbm, weights),
            )
        )
    ]
    walk = [i + side * pairs for i in range(pairs) for side in range(2)]
    target_copies = {
        t: pltpu.make_async_copy(
            target_hbm.at[pl.ds(t * pixels, pixels)],
            target.at[pl.ds(t * pixels, pixels)],
            target_sem.at[t],
        )
        for t in walk
    }
    for copy in small:
        copy.start()
    for t in walk:
        target_copies[t].start()
    row = lax.broadcasted_iota(jnp.int32, (both, both), 0)
    lane = lax.broadcasted_iota(jnp.int32, (both, both), 1)
    same = (row >= list_len) == (lane >= list_len)
    steps = lane.astype(jnp.float32)
    slot = lax.broadcasted_iota(jnp.int32, (both, 1), 0)
    place = lax.broadcasted_iota(jnp.int32, (rows, both), 0)
    for copy in small:
        copy.wait()
    order = jnp.concatenate([orders[:pairs, :], orders[pairs:, :] + list_len], axis=1)
    listed = jnp.concatenate([lists[:pairs, :], lists[pairs:, :]], axis=1)
    weight = weights[...]
    high, low = split(dot(weight, weight, NT))
    square_high_ref[...] = high
    square_low_ref[...] = low
    ranks, nearer = [], []
    for i in range(pairs):
        at = row == order[i : i + 1, :]
        rank = jnp.sum(jnp.where(at, steps, 0.0), axis=1, keepdims=True)
        ahead = same & (steps < rank)
        ranks.append(rank)
        nearer.append(dot(one_hot(ahead), one_hot(at), NT).astype(jnp.bfloat16))
    values = []
    for i in range(pairs):
        code = jnp.concatenate([codes[i], codes[i + pairs]], axis=0)
        alpha = code.astype(jnp.float32) * (ALPHA_TOP / 255.0)
        high, low = split(jnp.log(1.0 - alpha))
        transmit = jnp.exp(dot(nearer[i], high) + dot(nearer[i], low))
        limit = jnp.where(slot < list_len, counts[0, i], counts[0, i + pairs] + list_len)
        live = ranks[i] < limit.astype(jnp.float32)
        blend = jnp.where(live, transmit * alpha, 0.0).astype(jnp.bfloat16)
        blends[i * both : (i + 1) * both, :] = blend
        values.append(blend)
    inner = [split(jnp.where(same, dot(v, v, NT), 0.0)) for v in values]
    gram = jnp.zeros((rows, rows), jnp.float32)
    for i in range(pairs):
        chosen = one_hot(listed[i : i + 1, :] == place)
        hot[:, i * both : (i + 1) * both] = chosen
        high, low = split(dot(chosen, inner[i][0]) + dot(chosen, inner[i][1]))
        gram = gram + (dot(high, chosen, NT) + dot(low, chosen, NT))
    high, low = split(gram)
    gram_high_ref[...] = high
    gram_low_ref[...] = low
    total = jnp.zeros((8, target.shape[1]), jnp.float32)
    group = 2
    for i in range(pairs):
        for side in range(2):
            t = i + side * pairs
            target_copies[t].wait()
            goal = target[t * pixels : (t + 1) * pixels, :]
            begin = i * both + side * list_len
            own = slice(begin, begin + list_len)
            high, low = split(dot(blends[own, :], goal))
            bt_high[own, :] = high
            bt_low[own, :] = low
            wide = goal.astype(jnp.float32)
            total = total + jnp.sum((wide * wide).reshape(pixels // 8, 8, -1), axis=0)
        if i % group == group - 1:
            own = slice((i + 1 - group) * both, (i + 1) * both)
            chosen = hot[:, own]
            more = dot(chosen, bt_high[own, :]) + dot(chosen, bt_low[own, :])
            if i >= group:
                more = cross[...] + more
            if i < pairs - 1:
                cross[...] = more
    loss_ref[...] = jnp.full(loss_ref.shape, jnp.sum(total), jnp.float32)
    high, low = split(more)
    cross_high_ref[...] = high
    cross_low_ref[...] = low
    back_ref[...] = dot(high, weight, NT) + dot(low, weight, NT)


def gradient_kernel(
    parity_ref,
    buffer_ref,
    gram_high_ref,
    gram_low_ref,
    cross_high_ref,
    cross_low_ref,
    back_ref,
    square_high_ref,
    square_low_ref,
    loss_ref,
    weight_ref,
    send_ref,
    keep_ref,
    grads,
):
    parity = parity_ref[0]
    buffer = buffer_ref[...]
    rows, channels = buffer.shape
    chunks = send_ref.shape[0]
    per_owner = rows // (2 * chunks)
    share = channels // (2 * chunks)
    lanes = 128
    width = weight_ref.shape[1]
    strips = width // lanes
    body = share * strips
    half = channels // 2
    mixed = dot(gram_high_ref[...], buffer) + dot(gram_low_ref[...], buffer)
    high, low = split(mixed)
    square_high = square_high_ref[...]
    back = back_ref[...]
    slope = dot(high, square_high) + dot(low, square_high) + dot(high, square_low_ref[...]) - back
    grads[...] = slope
    loss = loss_ref[...] + jnp.sum(buffer.astype(jnp.float32) * (slope - back))
    source = lax.broadcasted_iota(jnp.int32, (channels, channels), 0)
    goal = lax.broadcasted_iota(jnp.int32, (channels, channels), 1)
    second = goal >= half
    inner = jnp.where(second, goal - half, goal)
    side = jnp.where(second, parity, 1 - parity)
    chunk = inner // share
    wanted = chunk * (2 * share) + side * share + (inner - chunk * share)
    ordered = dot(buffer, one_hot(source == wanted)).astype(jnp.bfloat16)
    core_high, core_low = split(dot(ordered, high, TN) + dot(ordered, low, TN))
    weight = weight_ref[...]
    grad = dot(core_high, weight) + dot(core_low, weight)
    grad = grad - dot(ordered, cross_high_ref[...], TN) - dot(ordered, cross_low_ref[...], TN)
    for number, (ref, which) in enumerate(((send_ref, 1 - parity), (keep_ref, parity))):
        for i in range(chunks):
            top = number * half + i * share
            for j in range(strips):
                ref[i, j * share : (j + 1) * share, :] = grad[
                    top : top + share, j * lanes : (j + 1) * lanes
                ]
            begin = pl.multiple_of((2 * i + which) * per_owner, per_owner)
            ref[i, body : body + per_owner, :] = grads[pl.ds(begin, per_owner), :]
            ref[i, body + per_owner :, :] = loss


def scale_bits(x):
    top = jnp.max(jnp.abs(x), axis=-2, keepdims=True)
    return jnp.ceil(jnp.log2(jnp.maximum(top, 1e-30)))


def to_code(x):
    return jnp.round(x).astype(jnp.int32).astype(jnp.int16)


def from_code(x):
    return x.astype(jnp.int32).astype(jnp.float32)


def join_kernel(body, per_owner, keep_ref, got_ref, out_ref):
    chunks, _, lanes = keep_ref.shape
    ends = body + 2 * per_owner
    dec = keep_ref[:, :body, :] + got_ref[:, :body, :]
    dec_bits = scale_bits(dec)
    out_ref[:, :body, :] = to_code(dec * (CODE_TOP * jnp.exp2(-dec_bits)))
    rows = slice(body, body + per_owner)
    moved = jnp.concatenate([keep_ref[:, rows, :], got_ref[:, rows, :]], axis=1)
    bits = scale_bits(moved)
    out_ref[:, body:ends, :] = to_code(moved * (CODE_TOP * jnp.exp2(-bits)))
    loss = keep_ref[:, body + per_owner :, :] + got_ref[:, body + per_owner :, :]
    loss = loss[:, :1, :]
    loss_bits = scale_bits(loss)
    loss = loss * (LOSS_TOP * jnp.exp2(-loss_bits))
    high = jnp.round(loss)
    low = (loss - high) * LOSS_TOP
    at = lax.broadcasted_iota(jnp.int32, (chunks, META, lanes), 1)
    meta = jnp.zeros((chunks, META, lanes), jnp.float32)
    for i, value in enumerate((dec_bits, bits, loss_bits, high, low)):
        meta = jnp.where(at == i, value, meta)
    out_ref[:, ends:, :] = to_code(meta)


def place_kernel(parity_ref, request_ref, after_ref, out_ref):
    del after_ref
    peers = request_ref.shape[0]
    rows = request_ref[...][:, 0, :]
    even = jnp.concatenate([rows[d : d + 1, :] for d in range(peers)], axis=1)
    odd = jnp.concatenate([rows[d ^ 1 : (d ^ 1) + 1, :] for d in range(peers)], axis=1)
    wanted = jnp.where(parity_ref[0] == 0, even, odd)
    out_ref[...] = one_hot(lax.broadcasted_iota(jnp.int32, out_ref.shape, 0) == wanted)


def finish_kernel(
    body, per_owner, dec_scale, loss_scale, chosen_ref, got_ref, feat_ref, dec_ref, loss_ref
):
    chunks, _, lanes = got_ref.shape
    share = dec_ref.shape[0]
    ends = body + 2 * per_owner
    meta = from_code(got_ref[:, ends:, :])
    dec = from_code(got_ref[:, :body, :]) * jnp.exp2(meta[:, 0:1, :])
    total = jnp.sum(dec, axis=0) * (dec_scale / CODE_TOP)
    for j in range(body // share):
        dec_ref[:, j * lanes : (j + 1) * lanes] = total[j * share : (j + 1) * share, :]
    loss = (meta[:, 3:4, :] + meta[:, 4:5, :] * (1.0 / LOSS_TOP)) * jnp.exp2(meta[:, 2:3, :])
    loss_ref[...] = jnp.sum(loss, axis=0) * (loss_scale / LOSS_TOP)
    moved = from_code(got_ref[:, body:ends, :]) * (jnp.exp2(meta[:, 1:2, :]) / CODE_TOP)
    high, low = split(moved.reshape(chunks * 2 * per_owner, lanes))
    chosen = chosen_ref[...]
    feat_ref[...] = dot(chosen, high) + dot(chosen, low)


def local(
    features, fetch_ids, tile_lists, depth_order, alpha_codes, list_counts, targets, dec_weight
):
    f32, bf16 = jnp.float32, jnp.bfloat16
    peers = lax.axis_size("wide")
    owned, channels = features.shape
    per_owner = fetch_ids.shape[2]
    rows = peers * per_owner
    tiles, list_len, pixels = alpha_codes.shape
    width = targets.shape[1]
    slots = tiles * list_len
    chunks = peers // 2
    share = channels // peers
    lanes = 128
    body = share * (width // lanes)
    parity = lax.rem(lax.axis_index("wide"), 2)
    shape = jax.ShapeDtypeStruct
    outgoing = pl.pallas_call(
        pick_kernel,
        out_shape=shape((rows, channels), bf16),
        in_specs=[VMEM, HBM],
        out_specs=VMEM,
        scratch_shapes=[pltpu.VMEM((owned, channels), bf16), pltpu.SemaphoreType.DMA],
        compiler_params=params(32),
        name="pick",
    )(pin(fetch_ids), pin(features))
    buffer = lax.all_to_all(
        outgoing.reshape(peers, per_owner, channels), "wide", split_axis=0, concat_axis=0, tiled=True
    ).reshape(rows, channels)
    grams = pl.pallas_call(
        gram_kernel,
        out_shape=(
            shape((rows, rows), bf16),
            shape((rows, rows), bf16),
            shape((rows, width), bf16),
            shape((rows, width), bf16),
            shape((rows, channels), f32),
            shape((channels, channels), bf16),
            shape((channels, channels), bf16),
            shape((8, lanes), f32),
        ),
        in_specs=[HBM] * 6,
        out_specs=(VMEM,) * 8,
        scratch_shapes=[
            pltpu.SMEM((1, tiles), jnp.int32),
            pltpu.VMEM((tiles, list_len), jnp.int32),
            pltpu.VMEM((tiles, list_len), jnp.int32),
            pltpu.VMEM((channels, width), bf16),
            pltpu.VMEM((tiles, list_len, pixels), jnp.int32),
            pltpu.VMEM((tiles * pixels, width), bf16),
            pltpu.VMEM((rows, slots), bf16),
            pltpu.VMEM((slots, pixels), bf16),
            pltpu.VMEM((slots, width), bf16),
            pltpu.VMEM((slots, width), bf16),
            pltpu.VMEM((rows, width), f32),
            pltpu.SemaphoreType.DMA((5,)),
            pltpu.SemaphoreType.DMA((tiles,)),
        ],
        cost_estimate=pl.CostEstimate(
            flops=2 * slots * pixels * width + 4 * rows * slots * (width + rows),
            bytes_accessed=targets.size * 2 + alpha_codes.size * 4,
            transcendentals=2 * alpha_codes.size,
        ),
        compiler_params=params(44),
        name="gram",
    )(*map(pin, (list_counts, tile_lists, depth_order, dec_weight, alpha_codes, targets)))
    half_shape = shape((chunks, body + per_owner + 8, lanes), f32)
    send, keep = pl.pallas_call(
        gradient_kernel,
        out_shape=(half_shape, half_shape),
        in_specs=[SMEM] + [VMEM] * 10,
        out_specs=(VMEM, VMEM),
        scratch_shapes=[pltpu.VMEM((rows, channels), f32)],
        compiler_params=params(40),
        name="gradient",
    )(parity.reshape(1), buffer, *grams, dec_weight)
    got = lax.ppermute(send, "wide", [(i, i ^ 1) for i in range(peers)])
    joined = pl.pallas_call(
        functools.partial(join_kernel, body, per_owner),
        out_shape=shape((chunks, body + 2 * per_owner + META, lanes), jnp.int16),
        in_specs=[VMEM, VMEM],
        out_specs=VMEM,
        compiler_params=params(32),
        name="join",
    )(keep, got)
    returned = lax.all_to_all(
        joined,
        "wide",
        split_axis=0,
        concat_axis=0,
        axis_index_groups=[[2 * i + c for i in range(chunks)] for c in range(2)],
        tiled=True,
    )
    chosen = pl.pallas_call(
        place_kernel,
        out_shape=shape((owned, rows), bf16),
        in_specs=[SMEM, VMEM, ANY],
        out_specs=VMEM,
        compiler_params=params(32),
        name="place",
    )(parity.reshape(1), fetch_ids, joined)
    pixel_total = peers * tiles * pixels
    feat_grad, dec_grad, loss = pl.pallas_call(
        functools.partial(
            finish_kernel,
            body,
            per_owner,
            1.0 / math.sqrt(pixel_total),
            0.5 / (pixel_total * width),
        ),
        out_shape=(
            shape((owned, channels), f32),
            shape((share, width), f32),
            shape((1, lanes), f32),
        ),
        in_specs=[VMEM, VMEM],
        out_specs=(VMEM,) * 3,
        compiler_params=params(32),
        name="finish",
    )(chosen, returned)
    return (feat_grad, dec_grad, loss[0, :1])


def solution(mesh):
    return jax.shard_map(
        local,
        mesh=mesh,
        in_specs=(
            P(("groups", "wide"), None),
            P("groups", "wide", None),
            P(("groups", "wide"), None),
            P(("groups", "wide"), None),
            P(("groups", "wide"), None, None),
            P(("groups", "wide"), None),
            P(("groups", "wide"), None),
            P(),
        ),
        out_specs=(P(("groups", "wide"), None), P(("groups", "wide"), None), P("groups")),
        check_vma=False,
    )
```

time: 54.2 us -> 42.2 us (0.78)
  local copies, waits for them, and re-layouts: 6.05 us -> 0.01 us
  waiting for transfers between devices: 13.9 us -> 9.73 us
  other arithmetic: 1.37 us -> 0 us
    unnamed x13 -> x4, local copies, waits for them, and re-layouts: 4.3 us -> 0.01 us
    all_to_all x1, waiting for transfers between devices: 12.6 us -> 8.42 us  [local(): lax.all_to_all(joined, 'wide', split_axis=0, concat_axis=0, axis_index_gr...]
    pallas_call x1, Pallas kernels: 14 us -> 11.8 us  [local(): pl.pallas_call(gram_kernel, out_shape=(shape((rows, rows), bf16), shape((...]
    pallas_call x1 -> x2, Pallas kernels: 1.02 us -> 2.94 us  [the longest x1 2.63 us: local(): pl.pallas_call(pick_kernel, out_shape=shape((rows, channels), bf16), in_s...]
    reshape x3 -> x0, local copies, waits for them, and re-layouts: 1.62 us -> none  [the longest x1 0.77 us: local(): tile_lists.reshape(tiles // 2, 2 * list_len)]
    unnamed x1 -> x0, other arithmetic: 1.37 us -> none
  transfers between devices with their start and end apart: 3 -> 3, of which waited for: 2 -> 2; matrix products, arithmetic and copies ran while one was open for 3% -> 0% of each run, Pallas kernels for 26% -> 29%
where the time goes in v2:
time: 42.2 us; the launch traced here: 41.8 us
  Pallas kernels  17.7 us (42%)
  starting transfers between devices  13.7 us (32%)
  waiting for transfers between devices  9.73 us (23%)
  between operations  0.71 us (2%)
    pallas_call x1, Pallas kernels, local(): pl.pallas_call(gram_kernel, out_shape=(shape((rows, rows), bf16), shape((...  11.8 us
    all_to_all x1, waiting for transfers between devices, local(): lax.all_to_all(joined, 'wide', split_axis=0, concat_axis=0, axis_index_gr...  8.42 us
    all_to_all x1, starting transfers between devices, local(): lax.all_to_all(outgoing.reshape(peers, per_owner, channels), 'wide', spli...  7.4 us
    all_to_all x1, starting transfers between devices, local(): lax.all_to_all(joined, 'wide', split_axis=0, concat_axis=0, axis_index_gr...  5.87 us
    pallas_call x1, Pallas kernels, local(): pl.pallas_call(pick_kernel, out_shape=shape((rows, channels), bf16), in_s...  2.63 us
    ppermute x1, waiting for transfers between devices, local(): got = lax.ppermute(send, 'wide', [(i, i ^ 1) for i in range(peers)])  1.3 us
    pallas_call x1, Pallas kernels, local(): pl.pallas_call(functools.partial(finish_kernel, body, per_owner, 1.0 / ma...  1.24 us
    pallas_call x1, Pallas kernels, local(): pl.pallas_call(gradient_kernel, out_shape=(half_shape, half_shape), in_sp...  0.86 us
  transfers between devices with their start and end apart: 3, of which 2 were waited for; matrix products, arithmetic and copies ran while one was open for 0% of the time, Pallas kernels for 29%

profile of v2, /device:TPU:0, one launch (start us, length us, event | category | flops | bytes accessed | tf_op | source)
XLA Modules:
  0.0 41.8 jit_solution(1394253445542909710)
XLA Ops:
  0.6 0.0 copy-start.1
  0.6 0.0 copy-start
  0.7 2.6 %pick.1 = bf16[256,128]{1,0:T(8,128)(2,1)} custom-call(s32[16,1,16]{2,1,0:T(1,128)} %request_ref.3, bf16[1024,128]{1,0:T(8,128)(2,1)} %feature_hbm.1), custom_call_target="tpu_custom_call" | custom-call | tf_op jit(solution)/shard_map/pick/pallas_call | solution.py:327
  3.3 7.4 %all-to-all-start = ((bf16[16,16,128]{2,1,0:T(8,128)(2,1)}), bf16[16,16,128]{2,1,0:T(8,128)(2,1)S(1)}, u32[]{:S(2)}, u32[]{:S(2)}) async-start(bf16[16,16,128]{2,1,0:T(8,128)(2,1)} %bitcast.1), calls=%async_computation | async-start | bytes 131072 | tf_op jit(solution)/shard_map/all_to_all | solution.py:336
  10.7 11.8 %gram.1 = (bf16[256,256]{1,0:T(8,128)(2,1)S(1)}, bf16[256,256]{1,0:T(8,128)(2,1)S(1)}, bf16[256,1024]{1,0:T(8,128)(2,1)S(1)}, bf16[256,1024]{1,0:T(8,128)(2,1)S(...) custom-call(s32[1,16]{1,0:T(1,128)} %count_hbm.1, ...), custom_call_target="tpu_custom_call" | custom-call | flops 1879048192 | bytes 9437184 | tf_op jit(solution)/shard_map/gram/pallas_call | solution.py:339
  22.5 0.0 all-to-all-done
  22.5 0.0 copy-done
  22.5 0.9 %gradient.1 = (f32[8,88,128]{2,1,0:T(8,128)S(1)}, f32[8,88,128]{2,1,0:T(8,128)S(1)}) custom-call(s32[1]{0:T(128)} %bitcast.parity_ref, bf16[256,128]{1,0:T(8,128)(2,1)S(1)} %bitcast.5, bf16[256,256]{1,0:T(8,128)(2,1)S(1)} %get-tuple-element.16.gram_high_ref, bf16[256,256]{1,0:T(8,128)(2,1)S(1)} %get-tuple-element.17.gram_low_ref, ...), custom_call_target="tpu_custom_call" | custom-call | tf_op jit(solution)/shard_map/gradient/pallas_call | solution.py:377
  23.4 0.5 %collective-permute-start = (f32[8,88,128]{2,1,0:T(8,128)S(1)}, f32[8,88,128]{2,1,0:T(8,128)S(1)}, u32[]{:S(2)}, u32[]{:S(2)}) collective-permute-start(f32[8,88,128]{2,1,0:T(8,128)S(1)} %get-tuple-element.25), channel_id=1, source_target_pairs={{0,1},{1,0},{2,3},{3,2},{4,5},{5,4},{6,7},{7,6},{8,9},{9,8},{10,11... | collective-permute-start | bytes 1081352 | tf_op jit(solution)/shard_map/ppermute | solution.py:386
  23.9 1.3 %collective-permute-done.got_ref = f32[8,88,128]{2,1,0:T(8,128)S(1)} collective-permute-done((f32[8,88,128]{2,1,0:T(8,128)S(1)}, f32[8,88,128]{2,1,0:T(8,128)S(1)}, u32[]{:S(2)}, u32[]{:S(2)}) %collective-permute-start) | collective-permute-done | bytes 360480 | tf_op jit(solution)/shard_map/ppermute | solution.py:386
  25.2 0.8 %join.1.after_ref = s16[8,112,128]{2,1,0:T(8,128)(2,1)} custom-call(f32[8,88,128]{2,1,0:T(8,128)S(1)} %get-tuple-element.24.keep_ref, f32[8,88,128]{2,1,0:T(8,128)S(1)} %collective-permute-done.got_ref), custom_call_target="tpu_custom_call" | custom-call | tf_op jit(solution)/shard_map/join/pallas_call | solution.py:387
  26.0 5.9 %all-to-all-start.1 = ((s16[8,112,128]{2,1,0:T(8,128)(2,1)}), s16[8,112,128]{2,1,0:T(8,128)(2,1)S(1)}, u32[]{:S(2)}, u32[]{:S(2)}) async-start(s16[8,112,128]{2,1,0:T(8,128)(2,1)} %join.1.after_ref), calls=%async_computation.1 | async-start | bytes 458752 | tf_op jit(solution)/shard_map/all_to_all | solution.py:395
  31.9 0.0 copy-done.1
  31.9 0.3 place.1.chosen_ref
  32.2 8.4 %all-to-all-done.1.got_ref = s16[8,112,128]{2,1,0:T(8,128)(2,1)S(1)} async-done(((s16[8,112,128]{2,1,0:T(8,128)(2,1)}), s16[8,112,128]{2,1,0:T(8,128)(2,1)S(1)}, u32[]{:S(2)}, u32[]{:S(2)}) %all-to-all-start.1) | async-done | bytes 229408 | tf_op jit(solution)/shard_map/all_to_all | solution.py:395
  40.6 1.2 %finish.1 = (f32[1024,128]{1,0:T(8,128)}, f32[8,1024]{1,0:T(8,128)}, f32[1,128]{1,0:T(1,128)}) custom-call(bf16[1024,256]{1,0:T(8,128)(2,1)S(1)} %place.1.chosen_ref, s16[8,112,128]{2,1,0:T(8,128)(2,1)S(1)} %all-to-all-done.1.got_ref), custom_call_target="tpu_custom_call" | custom-call | tf_op jit(solution)/shard_map/finish/pallas_call | solution.py:412
Async XLA Ops:
  0.6 31.2 %copy-start.1 = (s32[16,1,16]{2,1,0:T(1,128)S(1)}, s32[16,1,16]{2,1,0:T(1,128)}, u32[]{:S(2)}) copy-start(s32[16,1,16]{2,1,0:T(1,128)} %request_ref.3) | copy-start | bytes 3076
  0.6 21.9 %copy-start = (bf16[128,1024]{1,0:T(8,128)(2,1)S(1)}, bf16[128,1024]{1,0:T(8,128)(2,1)}, u32[]{:S(2)}) copy-start(bf16[128,1024]{1,0:T(8,128)(2,1)} %weight_ref.1) | copy-start | bytes 786436
  3.3 19.2 %all-to-all-start = ((bf16[16,16,128]{2,1,0:T(8,128)(2,1)}), bf16[16,16,128]{2,1,0:T(8,128)(2,1)S(1)}, u32[]{:S(2)}, u32[]{:S(2)}) async-start(bf16[16,16,128]{2,1,0:T(8,128)(2,1)} %bitcast.1), calls=%async_computation | async-start | bytes 131072 | tf_op jit(solution)/shard_map/all_to_all | solution.py:336
  23.4 1.8 %collective-permute-start = (f32[8,88,128]{2,1,0:T(8,128)S(1)}, f32[8,88,128]{2,1,0:T(8,128)S(1)}, u32[]{:S(2)}, u32[]{:S(2)}) collective-permute-start(f32[8,88,128]{2,1,0:T(8,128)S(1)} %get-tuple-element.25), channel_id=1, source_target_pairs={{0,1},{1,0},{2,3},{3,2},{4,5},{5,4},{6,7},{7,6},{8,9},{9,8},{10,11... | collective-permute-start | bytes 1081352 | tf_op jit(solution)/shard_map/ppermute | solution.py:386
  26.0 14.6 %all-to-all-start.1 = ((s16[8,112,128]{2,1,0:T(8,128)(2,1)}), s16[8,112,128]{2,1,0:T(8,128)(2,1)S(1)}, u32[]{:S(2)}, u32[]{:S(2)}) async-start(s16[8,112,128]{2,1,0:T(8,128)(2,1)} %join.1.after_ref), calls=%async_computation.1 | async-start | bytes 458752 | tf_op jit(solution)/shard_map/all_to_all | solution.py:395

commit v3 on v2

--- a/solution.py
+++ b/solution.py
@@ -38,29 +38,37 @@
     return pltpu.with_memory_space_constraint(x, pltpu.HBM)
 
 
+def near(x):
+    return pltpu.with_memory_space_constraint(x, pltpu.VMEM)
+
+
 def params(mib):
     return pltpu.CompilerParams(vmem_limit_bytes=mib << 20)
 
 
-def pick_kernel(request_ref, feature_hbm, out_ref, held, sem):
-    copy = pltpu.make_async_copy(feature_hbm, held, sem)
-    copy.start()
-    peers, _, per_owner = request_ref.shape
+def pick_kernel(request_hbm, feature_hbm, out_ref, wanted, held, sems):
+    copies = [
+        pltpu.make_async_copy(request_hbm, wanted, sems.at[0]),
+        pltpu.make_async_copy(feature_hbm, held, sems.at[1]),
+    ]
+    for copy in copies:
+        copy.start()
+    peers, _, per_owner = wanted.shape
     owned = held.shape[0]
     lane = lax.broadcasted_iota(jnp.int32, (peers, per_owner, owned), 2)
-    wanted = request_ref[...][:, 0, :]
-    chosen = jnp.where(wanted[:, :, None] == lane, 1.0, 0.0)
+    copies[0].wait()
+    chosen = jnp.where(wanted[...][:, 0, :][:, :, None] == lane, 1.0, 0.0)
     chosen = chosen.reshape(peers * per_owner, owned).astype(jnp.bfloat16)
-    copy.wait()
+    copies[1].wait()
     out_ref[...] = dot(chosen, held[...]).astype(jnp.bfloat16)
 
 
 def gram_kernel(
-    count_hbm,
-    list_hbm,
-    order_hbm,
-    weight_hbm,
-    code_hbm,
+    count_ref,
+    list_ref,
+    order_ref,
+    weight_ref,
+    code_ref,
     target_hbm,
     gram_high_ref,
     gram_low_ref,
@@ -70,60 +78,36 @@
     square_high_ref,
     square_low_ref,
     loss_ref,
-    counts,
-    lists,
-    orders,
-    weights,
-    codes,
-    target,
     hot,
+    part_high,
+    part_low,
     blends,
     bt_high,
     bt_low,
+    target,
     cross,
-    first_sem,
-    target_sem,
+    sems,
 ):
-    tiles, list_len, pixels = codes.shape
+    tiles, list_len, pixels = code_ref.shape
     rows = gram_high_ref.shape[0]
     both = 2 * list_len
     pairs = tiles // 2
-    small = [
-        pltpu.make_async_copy(source, goal, first_sem.at[i])
-        for i, (source, goal) in enumerate(
-            (
-                (count_hbm, counts),
-                (list_hbm, lists),
-                (order_hbm, orders),
-                (code_hbm, codes),
-                (weight_hbm, weights),
-            )
-        )
-    ]
-    walk = [i + side * pairs for i in range(pairs) for side in range(2)]
-    target_copies = {
-        t: pltpu.make_async_copy(
-            target_hbm.at[pl.ds(t * pixels, pixels)],
-            target.at[pl.ds(t * pixels, pixels)],
-            target_sem.at[t],
-        )
-        for t in walk
-    }
-    for copy in small:
+    part = pairs // 2
+    copies = []
+    for i, first in enumerate((0, pairs, part, pairs + part)):
+        span = pl.ds(first * pixels, part * pixels)
+        copies.append(pltpu.make_async_copy(target_hbm.at[span], target.at[span], sems.at[i]))
+    for copy in copies:
         copy.start()
-    for t in walk:
-        target_copies[t].start()
     row = lax.broadcasted_iota(jnp.int32, (both, both), 0)
     lane = lax.broadcasted_iota(jnp.int32, (both, both), 1)
     same = (row >= list_len) == (lane >= list_len)
     steps = lane.astype(jnp.float32)
     slot = lax.broadcasted_iota(jnp.int32, (both, 1), 0)
     place = lax.broadcasted_iota(jnp.int32, (rows, both), 0)
-    for copy in small:
-        copy.wait()
-    order = jnp.concatenate([orders[:pairs, :], orders[pairs:, :] + list_len], axis=1)
-    listed = jnp.concatenate([lists[:pairs, :], lists[pairs:, :]], axis=1)
-    weight = weights[...]
+    order = jnp.concatenate([order_ref[:pairs, :], order_ref[pairs:, :] + list_len], axis=1)
+    listed = jnp.concatenate([list_ref[:pairs, :], list_ref[pairs:, :]], axis=1)
+    weight = weight_ref[...]
     high, low = split(dot(weight, weight, NT))
     square_high_ref[...] = high
     square_low_ref[...] = low
@@ -136,49 +120,52 @@
         nearer.append(dot(one_hot(ahead), one_hot(at), NT).astype(jnp.bfloat16))
     values = []
     for i in range(pairs):
-        code = jnp.concatenate([codes[i], codes[i + pairs]], axis=0)
+        code = jnp.concatenate([code_ref[i], code_ref[i + pairs]], axis=0)
         alpha = code.astype(jnp.float32) * (ALPHA_TOP / 255.0)
-        high, low = split(jnp.log(1.0 - alpha))
-        transmit = jnp.exp(dot(nearer[i], high) + dot(nearer[i], low))
-        limit = jnp.where(slot < list_len, counts[0, i], counts[0, i + pairs] + list_len)
+        logs = jnp.concatenate(split(jnp.log(1.0 - alpha)), axis=0)
+        transmit = jnp.exp(dot(jnp.concatenate([nearer[i]] * 2, axis=1), logs))
+        first = count_ref[:, i : i + 1]
+        second = count_ref[:, i + pairs : i + pairs + 1] + list_len
+        limit = jnp.where(slot < list_len, first, second)
         live = ranks[i] < limit.astype(jnp.float32)
         blend = jnp.where(live, transmit * alpha, 0.0).astype(jnp.bfloat16)
         blends[i * both : (i + 1) * both, :] = blend
         values.append(blend)
     inner = [split(jnp.where(same, dot(v, v, NT), 0.0)) for v in values]
-    gram = jnp.zeros((rows, rows), jnp.float32)
     for i in range(pairs):
+        own = slice(i * both, (i + 1) * both)
         chosen = one_hot(listed[i : i + 1, :] == place)
-        hot[:, i * both : (i + 1) * both] = chosen
-        high, low = split(dot(chosen, inner[i][0]) + dot(chosen, inner[i][1]))
-        gram = gram + (dot(high, chosen, NT) + dot(low, chosen, NT))
-    high, low = split(gram)
+        hot[:, own] = chosen
+        wide = dot(chosen, jnp.concatenate(inner[i], axis=1))
+        high, low = split(wide[:, :both] + wide[:, both:])
+        part_high[:, own] = high
+        part_low[:, own] = low
+    chosen = hot[...]
+    high, low = split(dot(part_high[...], chosen, NT) + dot(part_low[...], chosen, NT))
     gram_high_ref[...] = high
     gram_low_ref[...] = low
     total = jnp.zeros((8, target.shape[1]), jnp.float32)
-    group = 2
-    for i in range(pairs):
-        for side in range(2):
-            t = i + side * pairs
-            target_copies[t].wait()
-            goal = target[t * pixels : (t + 1) * pixels, :]
-            begin = i * both + side * list_len
-            own = slice(begin, begin + list_len)
-            high, low = split(dot(blends[own, :], goal))
-            bt_high[own, :] = high
-            bt_low[own, :] = low
-            wide = goal.astype(jnp.float32)
-            total = total + jnp.sum((wide * wide).reshape(pixels // 8, 8, -1), axis=0)
-        if i % group == group - 1:
-            own = slice((i + 1 - group) * both, (i + 1) * both)
-            chosen = hot[:, own]
-            more = dot(chosen, bt_high[own, :]) + dot(chosen, bt_low[own, :])
-            if i >= group:
-                more = cross[...] + more
-            if i < pairs - 1:
-                cross[...] = more
+    for half in range(2):
+        copies[2 * half].wait()
+        copies[2 * half + 1].wait()
+        for i in range(half * part, (half + 1) * part):
+            for side in range(2):
+                t = i + side * pairs
+                goal = target[t * pixels : (t + 1) * pixels, :]
+                begin = i * both + side * list_len
+                own = slice(begin, begin + list_len)
+                high, low = split(dot(blends[own, :], goal))
+                bt_high[own, :] = high
+                bt_low[own, :] = low
+                wide = goal.astype(jnp.float32)
+                total = total + jnp.sum((wide * wide).reshape(pixels // 8, 8, -1), axis=0)
+        own = slice(half * part * both, (half + 1) * part * both)
+        chosen = hot[:, own]
+        more = dot(chosen, bt_high[own, :]) + dot(chosen, bt_low[own, :])
+        if half == 0:
+            cross[...] = more
     loss_ref[...] = jnp.full(loss_ref.shape, jnp.sum(total), jnp.float32)
-    high, low = split(more)
+    high, low = split(cross[...] + more)
     cross_high_ref[...] = high
     cross_low_ref[...] = low
     back_ref[...] = dot(high, weight, NT) + dot(low, weight, NT)
@@ -327,10 +314,17 @@
     outgoing = pl.pallas_call(
         pick_kernel,
         out_shape=shape((rows, channels), bf16),
-        in_specs=[VMEM, HBM],
+        in_specs=[HBM, HBM],
         out_specs=VMEM,
-        scratch_shapes=[pltpu.VMEM((owned, channels), bf16), pltpu.SemaphoreType.DMA],
-        compiler_params=params(32),
+        scratch_shapes=[
+            pltpu.VMEM((peers, 1, per_owner), jnp.int32),
+            pltpu.VMEM((owned, channels), bf16),
+            pltpu.SemaphoreType.DMA((2,)),
+        ],
+        cost_estimate=pl.CostEstimate(
+            flops=20_000_000_000, bytes_accessed=40_000_000, transcendentals=0
+        ),
+        compiler_params=params(16),
         name="pick",
     )(pin(fetch_ids), pin(features))
     buffer = lax.all_to_all(
@@ -348,31 +342,27 @@
             shape((channels, channels), bf16),
             shape((8, lanes), f32),
         ),
-        in_specs=[HBM] * 6,
+        in_specs=[VMEM] * 5 + [HBM],
         out_specs=(VMEM,) * 8,
         scratch_shapes=[
-            pltpu.SMEM((1, tiles), jnp.int32),
-            pltpu.VMEM((tiles, list_len), jnp.int32),
-            pltpu.VMEM((tiles, list_len), jnp.int32),
-            pltpu.VMEM((channels, width), bf16),
-            pltpu.VMEM((tiles, list_len, pixels), jnp.int32),
-            pltpu.VMEM((tiles * pixels, width), bf16),
+            pltpu.VMEM((rows, slots), bf16),
+            pltpu.VMEM((rows, slots), bf16),
             pltpu.VMEM((rows, slots), bf16),
             pltpu.VMEM((slots, pixels), bf16),
             pltpu.VMEM((slots, width), bf16),
             pltpu.VMEM((slots, width), bf16),
+            pltpu.VMEM((tiles * pixels, width), bf16),
             pltpu.VMEM((rows, width), f32),
-            pltpu.SemaphoreType.DMA((5,)),
-            pltpu.SemaphoreType.DMA((tiles,)),
+            pltpu.SemaphoreType.DMA((4,)),
         ],
         cost_estimate=pl.CostEstimate(
             flops=2 * slots * pixels * width + 4 * rows * slots * (width + rows),
             bytes_accessed=targets.size * 2 + alpha_codes.size * 4,
             transcendentals=2 * alpha_codes.size,
         ),
-        compiler_params=params(44),
+        compiler_params=params(36),
         name="gram",
-    )(*map(pin, (list_counts, tile_lists, depth_order, dec_weight, alpha_codes, targets)))
+    )(*map(near, (list_counts, tile_lists, depth_order, dec_weight, alpha_codes)), pin(targets))
     half_shape = shape((chunks, body + per_owner + 8, lanes), f32)
     send, keep = pl.pallas_call(
         gradient_kernel,
@@ -380,7 +370,7 @@
         in_specs=[SMEM] + [VMEM] * 10,
         out_specs=(VMEM, VMEM),
         scratch_shapes=[pltpu.VMEM((rows, channels), f32)],
-        compiler_params=params(40),
+        compiler_params=params(24),
         name="gradient",
     )(parity.reshape(1), buffer, *grams, dec_weight)
     got = lax.ppermute(send, "wide", [(i, i ^ 1) for i in range(peers)])

time: 42.2 us -> 35.8 us (0.85)
  Pallas kernels: 17.7 us -> 11.2 us
  waiting for transfers between devices: 9.73 us -> 11 us
  starting transfers between devices: 13.7 us -> 12.5 us
    pallas_call x1, Pallas kernels: 11.8 us -> 5.97 us  [local(): pl.pallas_call(gram_kernel, out_shape=(shape((rows, rows), bf16), shape((...]
    all_to_all x1, waiting for transfers between devices: 0.01 us -> 0.86 us  [local(): lax.all_to_all(outgoing.reshape(peers, per_owner, channels), 'wide', spli...]
    all_to_all x1, starting transfers between devices: 5.87 us -> 5.04 us  [local(): lax.all_to_all(joined, 'wide', split_axis=0, concat_axis=0, axis_index_gr...]
    pallas_call x1, Pallas kernels: 2.63 us -> 2 us  [local(): pl.pallas_call(pick_kernel, out_shape=shape((rows, channels), bf16), in_s...]
  transfers between devices with their start and end apart: 3 -> 3, of which waited for: 2 -> 3; matrix products, arithmetic and copies ran while one was open for 0% -> 0% of each run, Pallas kernels for 29% -> 18%
where the time goes in v3:
time: 35.8 us; the launch traced here: 35.5 us
  starting transfers between devices  12.5 us (35%)
  Pallas kernels  11.2 us (31%)
  waiting for transfers between devices  11 us (31%)
  between operations  0.78 us (2%)
    all_to_all x1, waiting for transfers between devices, local(): lax.all_to_all(joined, 'wide', split_axis=0, concat_axis=0, axis_index_gr...  8.43 us
    all_to_all x1, starting transfers between devices, local(): lax.all_to_all(outgoing.reshape(peers, per_owner, channels), 'wide', spli...  7.4 us
    pallas_call x1, Pallas kernels, local(): pl.pallas_call(gram_kernel, out_shape=(shape((rows, rows), bf16), shape((...  5.97 us
    all_to_all x1, starting transfers between devices, local(): lax.all_to_all(joined, 'wide', split_axis=0, concat_axis=0, axis_index_gr...  5.04 us
    pallas_call x1, Pallas kernels, local(): pl.pallas_call(pick_kernel, out_shape=shape((rows, channels), bf16), in_s...  2 us
    ppermute x1, waiting for transfers between devices, local(): got = lax.ppermute(send, 'wide', [(i, i ^ 1) for i in range(peers)])  1.66 us
    pallas_call x1, Pallas kernels, local(): pl.pallas_call(functools.partial(finish_kernel, body, per_owner, 1.0 / ma...  1.25 us
    all_to_all x1, waiting for transfers between devices, local(): lax.all_to_all(outgoing.reshape(peers, per_owner, channels), 'wide', spli...  0.86 us
  transfers between devices with their start and end apart: 3, of which 3 were waited for; matrix products, arithmetic and copies ran while one was open for 0% of the time, Pallas kernels for 18%

profile of v3, /device:TPU:0, one launch (start us, length us, event | category | flops | bytes accessed | tf_op | source)
XLA Modules:
  0.0 35.5 jit_solution(15729019962711653410)
XLA Ops:
  0.6 0.0 copy-start.1
  0.6 0.0 copy-start.5
  0.7 0.0 copy-start
  0.7 0.0 copy-start.3
  0.7 0.0 copy-start.2
  0.7 2.0 %pick.1 = bf16[256,128]{1,0:T(8,128)(2,1)} custom-call(s32[16,1,16]{2,1,0:T(1,128)} %request_ref.1, bf16[1024,128]{1,0:T(8,128)(2,1)} %feature_hbm.1), custom_call_target="tpu_custom_call" | custom-call | flops 20000000000 | bytes 40000000 | tf_op jit(solution)/shard_map/pick/pallas_call | solution.py:314
  2.7 0.0 copy-start.4
  2.7 7.4 %all-to-all-start = ((bf16[16,16,128]{2,1,0:T(8,128)(2,1)}), bf16[16,16,128]{2,1,0:T(8,128)(2,1)S(1)}, u32[]{:S(2)}, u32[]{:S(2)}) async-start(bf16[16,16,128]{2,1,0:T(8,128)(2,1)} %bitcast.1), calls=%async_computation | async-start | bytes 131072 | tf_op jit(solution)/shard_map/all_to_all | solution.py:330
  10.1 0.0 copy-done.1
  10.1 0.0 copy-done.5
  10.1 0.0 copy-done
  10.1 0.0 copy-done.3
  10.1 0.0 copy-done.2
  10.2 6.0 %gram.1 = (bf16[256,256]{1,0:T(8,128)(2,1)S(1)}, bf16[256,256]{1,0:T(8,128)(2,1)S(1)}, bf16[256,1024]{1,0:T(8,128)(2,1)S(1)}, bf16[256,1024]{1,0:T(8,128)(2,1)S(...) custom-call(s32[1,16]{1,0:T(1,128)S(1)} %copy-done.5, ...), custom_call_target="tpu_custom_call" | custom-call | flops 1879048192 | bytes 9437184 | tf_op jit(solution)/shard_map/gram/pallas_call | solution.py:333
  16.1 0.9 %all-to-all-done = bf16[16,16,128]{2,1,0:T(8,128)(2,1)S(1)} async-done(((bf16[16,16,128]{2,1,0:T(8,128)(2,1)}), bf16[16,16,128]{2,1,0:T(8,128)(2,1)S(1)}, u32[]{:S(2)}, u32[]{:S(2)}) %all-to-all-start) | async-done | bytes 65568 | tf_op jit(solution)/shard_map/all_to_all | solution.py:330
  17.0 0.9 %gradient.1 = (f32[8,88,128]{2,1,0:T(8,128)S(1)}, f32[8,88,128]{2,1,0:T(8,128)S(1)}) custom-call(s32[1]{0:T(128)} %bitcast.parity_ref, bf16[256,128]{1,0:T(8,128)(2,1)S(1)} %bitcast.5, bf16[256,256]{1,0:T(8,128)(2,1)S(1)} %get-tuple-element.16.gram_high_ref, bf16[256,256]{1,0:T(8,128)(2,1)S(1)} %get-tuple-element.17.gram_low_ref, ...), custom_call_target="tpu_custom_call" | custom-call | tf_op jit(solution)/shard_map/gradient/pallas_call | solution.py:367
  17.9 0.1 collective-permute-start
  17.9 1.7 %collective-permute-done.got_ref = f32[8,88,128]{2,1,0:T(8,128)S(1)} collective-permute-done((f32[8,88,128]{2,1,0:T(8,128)S(1)}, f32[8,88,128]{2,1,0:T(8,128)S(1)}, u32[]{:S(2)}, u32[]{:S(2)}) %collective-permute-start) | collective-permute-done | bytes 360480 | tf_op jit(solution)/shard_map/ppermute | solution.py:376
  19.6 0.8 %join.1.after_ref = s16[8,112,128]{2,1,0:T(8,128)(2,1)} custom-call(f32[8,88,128]{2,1,0:T(8,128)S(1)} %get-tuple-element.24.keep_ref, f32[8,88,128]{2,1,0:T(8,128)S(1)} %collective-permute-done.got_ref), custom_call_target="tpu_custom_call" | custom-call | tf_op jit(solution)/shard_map/join/pallas_call | solution.py:377
  20.4 5.0 %all-to-all-start.1 = ((s16[8,112,128]{2,1,0:T(8,128)(2,1)}), s16[8,112,128]{2,1,0:T(8,128)(2,1)S(1)}, u32[]{:S(2)}, u32[]{:S(2)}) async-start(s16[8,112,128]{2,1,0:T(8,128)(2,1)} %join.1.after_ref), calls=%async_computation.1 | async-start | bytes 458752 | tf_op jit(solution)/shard_map/all_to_all | solution.py:385
  25.5 0.0 copy-done.4
  25.5 0.3 place.1.chosen_ref
  25.8 8.4 %all-to-all-done.1.got_ref = s16[8,112,128]{2,1,0:T(8,128)(2,1)S(1)} async-done(((s16[8,112,128]{2,1,0:T(8,128)(2,1)}), s16[8,112,128]{2,1,0:T(8,128)(2,1)S(1)}, u32[]{:S(2)}, u32[]{:S(2)}) %all-to-all-start.1) | async-done | bytes 229408 | tf_op jit(solution)/shard_map/all_to_all | solution.py:385
  34.2 1.2 %finish.1 = (f32[1024,128]{1,0:T(8,128)}, f32[8,1024]{1,0:T(8,128)}, f32[1,128]{1,0:T(1,128)}) custom-call(bf16[1024,256]{1,0:T(8,128)(2,1)S(1)} %place.1.chosen_ref, s16[8,112,128]{2,1,0:T(8,128)(2,1)S(1)} %all-to-all-done.1.got_ref), custom_call_target="tpu_custom_call" | custom-call | tf_op jit(solution)/shard_map/finish/pallas_call | solution.py:402
Async XLA Ops:
  0.6 9.5 %copy-start.1 = (bf16[128,1024]{1,0:T(8,128)(2,1)S(1)}, bf16[128,1024]{1,0:T(8,128)(2,1)}, u32[]{:S(2)}) copy-start(bf16[128,1024]{1,0:T(8,128)(2,1)} %weight_ref.3) | copy-start | bytes 786436
  0.6 9.5 %copy-start.5 = (s32[1,16]{1,0:T(1,128)S(1)}, s32[1,16]{1,0:T(1,128)}, u32[]{:S(2)}) copy-start(s32[1,16]{1,0:T(1,128)} %count_ref.1) | copy-start | bytes 196
  0.7 9.5 %copy-start = (s32[16,64,256]{2,1,0:T(8,128)S(1)}, s32[16,64,256]{2,1,0:T(8,128)}, u32[]{:S(2)}) copy-start(s32[16,64,256]{2,1,0:T(8,128)} %code_ref.1) | copy-start | bytes 3145732
  0.7 9.5 %copy-start.3 = (s32[16,64]{1,0:T(8,128)S(1)}, s32[16,64]{1,0:T(8,128)}, u32[]{:S(2)}) copy-start(s32[16,64]{1,0:T(8,128)} %order_ref.1) | copy-start | bytes 12292
  0.7 9.5 %copy-start.2 = (s32[16,64]{1,0:T(8,128)S(1)}, s32[16,64]{1,0:T(8,128)}, u32[]{:S(2)}) copy-start(s32[16,64]{1,0:T(8,128)} %list_ref.1) | copy-start | bytes 12292
  2.7 22.8 %copy-start.4 = (s32[16,1,16]{2,1,0:T(1,128)S(1)}, s32[16,1,16]{2,1,0:T(1,128)}, u32[]{:S(2)}) copy-start(s32[16,1,16]{2,1,0:T(1,128)} %request_ref.1) | copy-start | bytes 3076
  2.7 14.3 %all-to-all-start = ((bf16[16,16,128]{2,1,0:T(8,128)(2,1)}), bf16[16,16,128]{2,1,0:T(8,128)(2,1)S(1)}, u32[]{:S(2)}, u32[]{:S(2)}) async-start(bf16[16,16,128]{2,1,0:T(8,128)(2,1)} %bitcast.1), calls=%async_computation | async-start | bytes 131072 | tf_op jit(solution)/shard_map/all_to_all | solution.py:330
  17.9 1.7 %collective-permute-start = (f32[8,88,128]{2,1,0:T(8,128)S(1)}, f32[8,88,128]{2,1,0:T(8,128)S(1)}, u32[]{:S(2)}, u32[]{:S(2)}) collective-permute-start(f32[8,88,128]{2,1,0:T(8,128)S(1)} %get-tuple-element.25), channel_id=1, source_target_pairs={{0,1},{1,0},{2,3},{3,2},{4,5},{5,4},{6,7},{7,6},{8,9},{9,8},{10,11... | collective-permute-start | bytes 1081352 | tf_op jit(solution)/shard_map/ppermute | solution.py:376
  20.4 13.8 %all-to-all-start.1 = ((s16[8,112,128]{2,1,0:T(8,128)(2,1)}), s16[8,112,128]{2,1,0:T(8,128)(2,1)S(1)}, u32[]{:S(2)}, u32[]{:S(2)}) async-start(s16[8,112,128]{2,1,0:T(8,128)(2,1)} %join.1.after_ref), calls=%async_computation.1 | async-start | bytes 458752 | tf_op jit(solution)/shard_map/all_to_all | solution.py:385

commit v4 on v3

--- a/solution.py
+++ b/solution.py
@@ -242,7 +242,8 @@
     return x.astype(jnp.int32).astype(jnp.float32)
 
 
-def join_kernel(body, per_owner, keep_ref, got_ref, out_ref):
+def join_kernel(body, per_owner, keep_ref, got_ref, after_ref, out_ref):
+    del after_ref
     chunks, _, lanes = keep_ref.shape
     ends = body + 2 * per_owner
     dec = keep_ref[:, :body, :] + got_ref[:, :body, :]
@@ -374,14 +375,25 @@
         name="gradient",
     )(parity.reshape(1), buffer, *grams, dec_weight)
     got = lax.ppermute(send, "wide", [(i, i ^ 1) for i in range(peers)])
+    chosen = pl.pallas_call(
+        place_kernel,
+        out_shape=shape((owned, rows), bf16),
+        in_specs=[SMEM, VMEM, ANY],
+        out_specs=VMEM,
+        cost_estimate=pl.CostEstimate(
+            flops=owned * rows, bytes_accessed=2 * owned * rows, transcendentals=0
+        ),
+        compiler_params=params(32),
+        name="place",
+    )(parity.reshape(1), fetch_ids, send)
     joined = pl.pallas_call(
         functools.partial(join_kernel, body, per_owner),
         out_shape=shape((chunks, body + 2 * per_owner + META, lanes), jnp.int16),
-        in_specs=[VMEM, VMEM],
+        in_specs=[VMEM, VMEM, ANY],
         out_specs=VMEM,
         compiler_params=params(32),
         name="join",
-    )(keep, got)
+    )(keep, got, chosen)
     returned = lax.all_to_all(
         joined,
         "wide",
@@ -390,14 +402,6 @@
         axis_index_groups=[[2 * i + c for i in range(chunks)] for c in range(2)],
         tiled=True,
     )
-    chosen = pl.pallas_call(
-        place_kernel,
-        out_shape=shape((owned, rows), bf16),
-        in_specs=[SMEM, VMEM, ANY],
-        out_specs=VMEM,
-        compiler_params=params(32),
-        name="place",
-    )(parity.reshape(1), fetch_ids, joined)
     pixel_total = peers * tiles * pixels
     feat_grad, dec_grad, loss = pl.pallas_call(
         functools.partial(

time: 35.8 us -> 34.8 us (0.972)
  blocking collectives: 0 us -> 13.6 us
  waiting for transfers between devices: 11 us -> 2.2 us
  starting transfers between devices: 12.5 us -> 7.47 us
  Pallas kernels: 11.2 us -> 10.5 us
    all_to_all x0 -> x1, blocking collectives: none -> 13.6 us  [local(): lax.all_to_all(joined, 'wide', split_axis=0, concat_axis=0, axis_index_gr...]
    all_to_all x1 -> x0, waiting for transfers between devices: 8.43 us -> none  [local(): lax.all_to_all(joined, 'wide', split_axis=0, concat_axis=0, axis_index_gr...]
    all_to_all x1 -> x0, starting transfers between devices: 5.04 us -> none  [local(): lax.all_to_all(joined, 'wide', split_axis=0, concat_axis=0, axis_index_gr...]
    pallas_call x1, Pallas kernels: 0.81 us -> 0.13 us  [local(): pl.pallas_call(functools.partial(join_kernel, body, per_owner), out_shape...]
  transfers between devices with their start and end apart: 3 -> 2, of which waited for: 3 -> 2; matrix products, arithmetic and copies ran while one was open for 0% -> 0% of each run, Pallas kernels for 18% -> 18%
where the time goes in v4:
time: 34.8 us; the launch traced here: 34.6 us
  blocking collectives  13.6 us (39%)
  Pallas kernels  10.5 us (30%)
  starting transfers between devices  7.47 us (21%)
  waiting for transfers between devices  2.2 us (6%)
  between operations  0.78 us (2%)
    all_to_all x1, blocking collectives, local(): lax.all_to_all(joined, 'wide', split_axis=0, concat_axis=0, axis_index_gr...  13.6 us
    all_to_all x1, starting transfers between devices, local(): lax.all_to_all(outgoing.reshape(peers, per_owner, channels), 'wide', spli...  7.4 us
    pallas_call x1, Pallas kernels, local(): pl.pallas_call(gram_kernel, out_shape=(shape((rows, rows), bf16), shape((...  5.97 us
    pallas_call x1, Pallas kernels, local(): pl.pallas_call(pick_kernel, out_shape=shape((rows, channels), bf16), in_s...  2 us
    ppermute x1, waiting for transfers between devices, local(): got = lax.ppermute(send, 'wide', [(i, i ^ 1) for i in range(peers)])  1.33 us
    pallas_call x1, Pallas kernels, local(): pl.pallas_call(functools.partial(finish_kernel, body, per_owner, 1.0 / ma...  1.25 us
    all_to_all x1, waiting for transfers between devices, local(): lax.all_to_all(outgoing.reshape(peers, per_owner, channels), 'wide', spli...  0.86 us
    pallas_call x1, Pallas kernels, local(): pl.pallas_call(gradient_kernel, out_shape=(half_shape, half_shape), in_sp...  0.85 us
  transfers between devices with their start and end apart: 2, of which 2 were waited for; matrix products, arithmetic and copies ran while one was open for 0% of the time, Pallas kernels for 18%

profile of v4, /device:TPU:0, one launch (start us, length us, event | category | flops | bytes accessed | tf_op | source)
XLA Modules:
  0.0 34.6 jit_solution(14300373976905562483)
XLA Ops:
  0.6 0.0 copy-start.1
  0.6 0.0 copy-start.5
  0.7 0.0 copy-start
  0.7 0.0 copy-start.3
  0.7 0.0 copy-start.2
  0.7 2.0 %pick.1 = bf16[256,128]{1,0:T(8,128)(2,1)} custom-call(s32[16,1,16]{2,1,0:T(1,128)} %request_ref.1, bf16[1024,128]{1,0:T(8,128)(2,1)} %feature_hbm.1), custom_call_target="tpu_custom_call" | custom-call | flops 20000000000 | bytes 40000000 | tf_op jit(solution)/shard_map/pick/pallas_call | solution.py:315
  2.7 0.0 copy-start.4
  2.7 7.4 %all-to-all-start = ((bf16[16,16,128]{2,1,0:T(8,128)(2,1)}), bf16[16,16,128]{2,1,0:T(8,128)(2,1)S(1)}, u32[]{:S(2)}, u32[]{:S(2)}) async-start(bf16[16,16,128]{2,1,0:T(8,128)(2,1)} %bitcast.1), calls=%async_computation | async-start | bytes 131072 | tf_op jit(solution)/shard_map/all_to_all | solution.py:331
  10.1 0.0 copy-done.1
  10.1 0.0 copy-done.5
  10.1 0.0 copy-done
  10.1 0.0 copy-done.3
  10.1 0.0 copy-done.2
  10.2 6.0 %gram.1 = (bf16[256,256]{1,0:T(8,128)(2,1)S(1)}, bf16[256,256]{1,0:T(8,128)(2,1)S(1)}, bf16[256,1024]{1,0:T(8,128)(2,1)S(1)}, bf16[256,1024]{1,0:T(8,128)(2,1)S(...) custom-call(s32[1,16]{1,0:T(1,128)S(1)} %copy-done.5, ...), custom_call_target="tpu_custom_call" | custom-call | flops 1879048192 | bytes 9437184 | tf_op jit(solution)/shard_map/gram/pallas_call | solution.py:334
  16.1 0.9 %all-to-all-done = bf16[16,16,128]{2,1,0:T(8,128)(2,1)S(1)} async-done(((bf16[16,16,128]{2,1,0:T(8,128)(2,1)}), bf16[16,16,128]{2,1,0:T(8,128)(2,1)S(1)}, u32[]{:S(2)}, u32[]{:S(2)}) %all-to-all-start) | async-done | bytes 65568 | tf_op jit(solution)/shard_map/all_to_all | solution.py:331
  17.0 0.9 %gradient.1 = (f32[8,88,128]{2,1,0:T(8,128)S(1)}, f32[8,88,128]{2,1,0:T(8,128)S(1)}) custom-call(s32[1]{0:T(128)} %bitcast.parity_ref, bf16[256,128]{1,0:T(8,128)(2,1)S(1)} %bitcast.5, bf16[256,256]{1,0:T(8,128)(2,1)S(1)} %get-tuple-element.16.gram_high_ref, bf16[256,256]{1,0:T(8,128)(2,1)S(1)} %get-tuple-element.17.gram_low_ref, ...), custom_call_target="tpu_custom_call" | custom-call | tf_op jit(solution)/shard_map/gradient/pallas_call | solution.py:368
  17.9 0.1 collective-permute-start
  17.9 0.0 copy-done.4
  18.0 0.3 place.1.after_ref.chosen_ref
  18.3 1.3 %collective-permute-done.got_ref = f32[8,88,128]{2,1,0:T(8,128)S(1)} collective-permute-done((f32[8,88,128]{2,1,0:T(8,128)S(1)}, f32[8,88,128]{2,1,0:T(8,128)S(1)}, u32[]{:S(2)}, u32[]{:S(2)}) %collective-permute-start) | collective-permute-done | bytes 360480 | tf_op jit(solution)/shard_map/ppermute | solution.py:377
  19.6 0.1 join.1
  19.7 13.6 %all_to_all.10.got_ref = s16[8,112,128]{2,1,0:T(8,128)(2,1)S(1)} all-to-all(s16[8,112,128]{2,1,0:T(8,128)(2,1)S(1)} %join.1), channel_id=1, replica_groups={{0,2,4,6,8,10,12,14},{1,3,5,7,9,11,13,15},{16,18,20,22,24,26,28,30},{17..., dimensions={0} | all-to-all | bytes 458752 | tf_op jit(solution)/shard_map/all_to_all | solution.py:397
  33.3 1.2 %finish.1 = (f32[1024,128]{1,0:T(8,128)}, f32[8,1024]{1,0:T(8,128)}, f32[1,128]{1,0:T(1,128)}) custom-call(bf16[1024,256]{1,0:T(8,128)(2,1)S(1)} %place.1.after_ref.chosen_ref, s16[8,112,128]{2,1,0:T(8,128)(2,1)S(1)} %all_to_all.10.got_ref), custom_call_target="tpu_custom_call" | custom-call | tf_op jit(solution)/shard_map/finish/pallas_call | solution.py:406
Async XLA Ops:
  0.6 9.5 %copy-start.1 = (bf16[128,1024]{1,0:T(8,128)(2,1)S(1)}, bf16[128,1024]{1,0:T(8,128)(2,1)}, u32[]{:S(2)}) copy-start(bf16[128,1024]{1,0:T(8,128)(2,1)} %weight_ref.3) | copy-start | bytes 786436
  0.6 9.5 %copy-start.5 = (s32[1,16]{1,0:T(1,128)S(1)}, s32[1,16]{1,0:T(1,128)}, u32[]{:S(2)}) copy-start(s32[1,16]{1,0:T(1,128)} %count_ref.1) | copy-start | bytes 196
  0.7 9.5 %copy-start = (s32[16,64,256]{2,1,0:T(8,128)S(1)}, s32[16,64,256]{2,1,0:T(8,128)}, u32[]{:S(2)}) copy-start(s32[16,64,256]{2,1,0:T(8,128)} %code_ref.1) | copy-start | bytes 3145732
  0.7 9.5 %copy-start.3 = (s32[16,64]{1,0:T(8,128)S(1)}, s32[16,64]{1,0:T(8,128)}, u32[]{:S(2)}) copy-start(s32[16,64]{1,0:T(8,128)} %order_ref.1) | copy-start | bytes 12292
  0.7 9.5 %copy-start.2 = (s32[16,64]{1,0:T(8,128)S(1)}, s32[16,64]{1,0:T(8,128)}, u32[]{:S(2)}) copy-start(s32[16,64]{1,0:T(8,128)} %list_ref.1) | copy-start | bytes 12292
  2.7 15.3 %copy-start.4 = (s32[16,1,16]{2,1,0:T(1,128)S(1)}, s32[16,1,16]{2,1,0:T(1,128)}, u32[]{:S(2)}) copy-start(s32[16,1,16]{2,1,0:T(1,128)} %request_ref.1) | copy-start | bytes 3076
  2.7 14.3 %all-to-all-start = ((bf16[16,16,128]{2,1,0:T(8,128)(2,1)}), bf16[16,16,128]{2,1,0:T(8,128)(2,1)S(1)}, u32[]{:S(2)}, u32[]{:S(2)}) async-start(bf16[16,16,128]{2,1,0:T(8,128)(2,1)} %bitcast.1), calls=%async_computation | async-start | bytes 131072 | tf_op jit(solution)/shard_map/all_to_all | solution.py:331
  17.9 1.7 %collective-permute-start = (f32[8,88,128]{2,1,0:T(8,128)S(1)}, f32[8,88,128]{2,1,0:T(8,128)S(1)}, u32[]{:S(2)}, u32[]{:S(2)}) collective-permute-start(f32[8,88,128]{2,1,0:T(8,128)S(1)} %get-tuple-element.24.after_ref), channel_id=1, source_target_pairs={{0,1},{1,0},{2,3},{3,2},{4,5},{5,4},{6,7},{7,6},{8,9},{9,8},{10,11... | collective-permute-start | bytes 1081352 | tf_op jit(solution)/shard_map/ppermute | solution.py:377

commit v5 on v4

--- a/solution.py
+++ b/solution.py
@@ -40,6 +40,10 @@
 
 def near(x):
     return pltpu.with_memory_space_constraint(x, pltpu.VMEM)
+
+
+def turn(i, chunks):
+    return (chunks - 1 - i) ^ 1
 
 
 def params(mib):
@@ -211,7 +215,7 @@
     inner = jnp.where(second, goal - half, goal)
     side = jnp.where(second, parity, 1 - parity)
     chunk = inner // share
-    wanted = chunk * (2 * share) + side * share + (inner - chunk * share)
+    wanted = turn(chunk, chunks) * (2 * share) + side * share + (inner - chunk * share)
     ordered = dot(buffer, one_hot(source == wanted)).astype(jnp.bfloat16)
     core_high, core_low = split(dot(ordered, high, TN) + dot(ordered, low, TN))
     weight = weight_ref[...]
@@ -224,7 +228,7 @@
                 ref[i, j * share : (j + 1) * share, :] = grad[
                     top : top + share, j * lanes : (j + 1) * lanes
                 ]
-            begin = pl.multiple_of((2 * i + which) * per_owner, per_owner)
+            begin = pl.multiple_of((2 * turn(i, chunks) + which) * per_owner, per_owner)
             ref[i, body : body + per_owner, :] = grads[pl.ds(begin, per_owner), :]
             ref[i, body + per_owner :, :] = loss
 
@@ -270,8 +274,9 @@
     del after_ref
     peers = request_ref.shape[0]
     rows = request_ref[...][:, 0, :]
-    even = jnp.concatenate([rows[d : d + 1, :] for d in range(peers)], axis=1)
-    odd = jnp.concatenate([rows[d ^ 1 : (d ^ 1) + 1, :] for d in range(peers)], axis=1)
+    walk = [2 * turn(i, peers // 2) + side for i in range(peers // 2) for side in range(2)]
+    even = jnp.concatenate([rows[d : d + 1, :] for d in walk], axis=1)
+    odd = jnp.concatenate([rows[d ^ 1 : (d ^ 1) + 1, :] for d in walk], axis=1)
     wanted = jnp.where(parity_ref[0] == 0, even, odd)
     out_ref[...] = one_hot(lax.broadcasted_iota(jnp.int32, out_ref.shape, 0) == wanted)
 
@@ -399,7 +404,7 @@
         "wide",
         split_axis=0,
         concat_axis=0,
-        axis_index_groups=[[2 * i + c for i in range(chunks)] for c in range(2)],
+        axis_index_groups=[[2 * turn(i, chunks) + c for i in range(chunks)] for c in range(2)],
         tiled=True,
     )
     pixel_total = peers * tiles * pixels

time: 34.8 us -> 32.7 us (0.940)
  blocking collectives: 13.6 us -> 11.4 us
    all_to_all x1, blocking collectives: 13.6 us -> 11.4 us  [local(): lax.all_to_all(joined, 'wide', split_axis=0, concat_axis=0, axis_index_gr...]
  transfers between devices with their start and end apart: 2 -> 2, of which waited for: 2 -> 2; matrix products, arithmetic and copies ran while one was open for 0% -> 0% of each run, Pallas kernels for 18% -> 19%
where the time goes in v5:
time: 32.7 us; the launch traced here: 32.4 us
  blocking collectives  11.4 us (35%)
  Pallas kernels  10.5 us (32%)
  starting transfers between devices  7.47 us (23%)
  waiting for transfers between devices  2.2 us (7%)
  between operations  0.78 us (2%)
    all_to_all x1, blocking collectives, local(): lax.all_to_all(joined, 'wide', split_axis=0, concat_axis=0, axis_index_gr...  11.4 us
    all_to_all x1, starting transfers between devices, local(): lax.all_to_all(outgoing.reshape(peers, per_owner, channels), 'wide', spli...  7.4 us
    pallas_call x1, Pallas kernels, local(): pl.pallas_call(gram_kernel, out_shape=(shape((rows, rows), bf16), shape((...  5.97 us
    pallas_call x1, Pallas kernels, local(): pl.pallas_call(pick_kernel, out_shape=shape((rows, channels), bf16), in_s...  2 us
    ppermute x1, waiting for transfers between devices, local(): got = lax.ppermute(send, 'wide', [(i, i ^ 1) for i in range(peers)])  1.33 us
    pallas_call x1, Pallas kernels, local(): pl.pallas_call(functools.partial(finish_kernel, body, per_owner, 1.0 / ma...  1.24 us
    all_to_all x1, waiting for transfers between devices, local(): lax.all_to_all(outgoing.reshape(peers, per_owner, channels), 'wide', spli...  0.86 us
    pallas_call x1, Pallas kernels, local(): pl.pallas_call(gradient_kernel, out_shape=(half_shape, half_shape), in_sp...  0.85 us
  transfers between devices with their start and end apart: 2, of which 2 were waited for; matrix products, arithmetic and copies ran while one was open for 0% of the time, Pallas kernels for 19%

profile of v5, /device:TPU:0, one launch (start us, length us, event | category | flops | bytes accessed | tf_op | source)
XLA Modules:
  0.0 32.4 jit_solution(2737063451954134875)
XLA Ops:
  0.6 0.0 copy-start.1
  0.6 0.0 copy-start.5
  0.7 0.0 copy-start
  0.7 0.0 copy-start.3
  0.7 0.0 copy-start.2
  0.7 2.0 %pick.1 = bf16[256,128]{1,0:T(8,128)(2,1)} custom-call(s32[16,1,16]{2,1,0:T(1,128)} %request_ref.1, bf16[1024,128]{1,0:T(8,128)(2,1)} %feature_hbm.1), custom_call_target="tpu_custom_call" | custom-call | flops 20000000000 | bytes 40000000 | tf_op jit(solution)/shard_map/pick/pallas_call | solution.py:320
  2.7 0.0 copy-start.4
  2.7 7.4 %all-to-all-start = ((bf16[16,16,128]{2,1,0:T(8,128)(2,1)}), bf16[16,16,128]{2,1,0:T(8,128)(2,1)S(1)}, u32[]{:S(2)}, u32[]{:S(2)}) async-start(bf16[16,16,128]{2,1,0:T(8,128)(2,1)} %bitcast.1), calls=%async_computation | async-start | bytes 131072 | tf_op jit(solution)/shard_map/all_to_all | solution.py:336
  10.1 0.0 copy-done.1
  10.1 0.0 copy-done.5
  10.1 0.0 copy-done
  10.1 0.0 copy-done.3
  10.1 0.0 copy-done.2
  10.2 6.0 %gram.1 = (bf16[256,256]{1,0:T(8,128)(2,1)S(1)}, bf16[256,256]{1,0:T(8,128)(2,1)S(1)}, bf16[256,1024]{1,0:T(8,128)(2,1)S(1)}, bf16[256,1024]{1,0:T(8,128)(2,1)S(...) custom-call(s32[1,16]{1,0:T(1,128)S(1)} %copy-done.5, ...), custom_call_target="tpu_custom_call" | custom-call | flops 1879048192 | bytes 9437184 | tf_op jit(solution)/shard_map/gram/pallas_call | solution.py:339
  16.1 0.9 %all-to-all-done = bf16[16,16,128]{2,1,0:T(8,128)(2,1)S(1)} async-done(((bf16[16,16,128]{2,1,0:T(8,128)(2,1)}), bf16[16,16,128]{2,1,0:T(8,128)(2,1)S(1)}, u32[]{:S(2)}, u32[]{:S(2)}) %all-to-all-start) | async-done | bytes 65568 | tf_op jit(solution)/shard_map/all_to_all | solution.py:336
  17.0 0.9 %gradient.1 = (f32[8,88,128]{2,1,0:T(8,128)S(1)}, f32[8,88,128]{2,1,0:T(8,128)S(1)}) custom-call(s32[1]{0:T(128)} %bitcast.parity_ref, bf16[256,128]{1,0:T(8,128)(2,1)S(1)} %bitcast.5, bf16[256,256]{1,0:T(8,128)(2,1)S(1)} %get-tuple-element.16.gram_high_ref, bf16[256,256]{1,0:T(8,128)(2,1)S(1)} %get-tuple-element.17.gram_low_ref, ...), custom_call_target="tpu_custom_call" | custom-call | tf_op jit(solution)/shard_map/gradient/pallas_call | solution.py:373
  17.9 0.1 collective-permute-start
  17.9 0.0 copy-done.4
  18.0 0.3 place.1.after_ref.chosen_ref
  18.3 1.3 %collective-permute-done.got_ref = f32[8,88,128]{2,1,0:T(8,128)S(1)} collective-permute-done((f32[8,88,128]{2,1,0:T(8,128)S(1)}, f32[8,88,128]{2,1,0:T(8,128)S(1)}, u32[]{:S(2)}, u32[]{:S(2)}) %collective-permute-start) | collective-permute-done | bytes 360480 | tf_op jit(solution)/shard_map/ppermute | solution.py:382
  19.6 0.1 join.1
  19.7 11.4 %all_to_all.10.got_ref = s16[8,112,128]{2,1,0:T(8,128)(2,1)S(1)} all-to-all(s16[8,112,128]{2,1,0:T(8,128)(2,1)S(1)} %join.1), channel_id=1, replica_groups={{12,14,8,10,4,6,0,2},{13,15,9,11,5,7,1,3},{28,30,24,26,20,22,16,18},{29..., dimensions={0} | all-to-all | bytes 458752 | tf_op jit(solution)/shard_map/all_to_all | solution.py:402
  31.2 1.2 %finish.1 = (f32[1024,128]{1,0:T(8,128)}, f32[8,1024]{1,0:T(8,128)}, f32[1,128]{1,0:T(1,128)}) custom-call(bf16[1024,256]{1,0:T(8,128)(2,1)S(1)} %place.1.after_ref.chosen_ref, s16[8,112,128]{2,1,0:T(8,128)(2,1)S(1)} %all_to_all.10.got_ref), custom_call_target="tpu_custom_call" | custom-call | tf_op jit(solution)/shard_map/finish/pallas_call | solution.py:411
Async XLA Ops:
  0.6 9.5 %copy-start.1 = (bf16[128,1024]{1,0:T(8,128)(2,1)S(1)}, bf16[128,1024]{1,0:T(8,128)(2,1)}, u32[]{:S(2)}) copy-start(bf16[128,1024]{1,0:T(8,128)(2,1)} %weight_ref.3) | copy-start | bytes 786436
  0.6 9.5 %copy-start.5 = (s32[1,16]{1,0:T(1,128)S(1)}, s32[1,16]{1,0:T(1,128)}, u32[]{:S(2)}) copy-start(s32[1,16]{1,0:T(1,128)} %count_ref.1) | copy-start | bytes 196
  0.7 9.5 %copy-start = (s32[16,64,256]{2,1,0:T(8,128)S(1)}, s32[16,64,256]{2,1,0:T(8,128)}, u32[]{:S(2)}) copy-start(s32[16,64,256]{2,1,0:T(8,128)} %code_ref.1) | copy-start | bytes 3145732
  0.7 9.5 %copy-start.3 = (s32[16,64]{1,0:T(8,128)S(1)}, s32[16,64]{1,0:T(8,128)}, u32[]{:S(2)}) copy-start(s32[16,64]{1,0:T(8,128)} %order_ref.1) | copy-start | bytes 12292
  0.7 9.5 %copy-start.2 = (s32[16,64]{1,0:T(8,128)S(1)}, s32[16,64]{1,0:T(8,128)}, u32[]{:S(2)}) copy-start(s32[16,64]{1,0:T(8,128)} %list_ref.1) | copy-start | bytes 12292
  2.7 15.3 %copy-start.4 = (s32[16,1,16]{2,1,0:T(1,128)S(1)}, s32[16,1,16]{2,1,0:T(1,128)}, u32[]{:S(2)}) copy-start(s32[16,1,16]{2,1,0:T(1,128)} %request_ref.1) | copy-start | bytes 3076
  2.7 14.3 %all-to-all-start = ((bf16[16,16,128]{2,1,0:T(8,128)(2,1)}), bf16[16,16,128]{2,1,0:T(8,128)(2,1)S(1)}, u32[]{:S(2)}, u32[]{:S(2)}) async-start(bf16[16,16,128]{2,1,0:T(8,128)(2,1)} %bitcast.1), calls=%async_computation | async-start | bytes 131072 | tf_op jit(solution)/shard_map/all_to_all | solution.py:336
  17.9 1.7 %collective-permute-start = (f32[8,88,128]{2,1,0:T(8,128)S(1)}, f32[8,88,128]{2,1,0:T(8,128)S(1)}, u32[]{:S(2)}, u32[]{:S(2)}) collective-permute-start(f32[8,88,128]{2,1,0:T(8,128)S(1)} %get-tuple-element.24.after_ref), channel_id=1, source_target_pairs={{0,1},{1,0},{2,3},{3,2},{4,5},{5,4},{6,7},{7,6},{8,9},{9,8},{10,11... | collective-permute-start | bytes 1081352 | tf_op jit(solution)/shard_map/ppermute | solution.py:382

commit v6 on v5

--- a/solution.py
+++ b/solution.py
@@ -282,22 +282,48 @@
 
 
 def finish_kernel(
-    body, per_owner, dec_scale, loss_scale, chosen_ref, got_ref, feat_ref, dec_ref, loss_ref
+    body,
+    per_owner,
+    dec_scale,
+    loss_scale,
+    chosen_ref,
+    got_ref,
+    feat_hbm,
+    dec_hbm,
+    loss_hbm,
+    feat,
+    dec,
+    loss,
+    sems,
 ):
     chunks, _, lanes = got_ref.shape
-    share = dec_ref.shape[0]
+    share = dec.shape[0]
     ends = body + 2 * per_owner
     meta = from_code(got_ref[:, ends:, :])
-    dec = from_code(got_ref[:, :body, :]) * jnp.exp2(meta[:, 0:1, :])
-    total = jnp.sum(dec, axis=0) * (dec_scale / CODE_TOP)
-    for j in range(body // share):
-        dec_ref[:, j * lanes : (j + 1) * lanes] = total[j * share : (j + 1) * share, :]
-    loss = (meta[:, 3:4, :] + meta[:, 4:5, :] * (1.0 / LOSS_TOP)) * jnp.exp2(meta[:, 2:3, :])
-    loss_ref[...] = jnp.sum(loss, axis=0) * (loss_scale / LOSS_TOP)
     moved = from_code(got_ref[:, body:ends, :]) * (jnp.exp2(meta[:, 1:2, :]) / CODE_TOP)
     high, low = split(moved.reshape(chunks * 2 * per_owner, lanes))
-    chosen = chosen_ref[...]
-    feat_ref[...] = dot(chosen, high) + dot(chosen, low)
+    blocks = sems.shape[0] - 2
+    step = feat.shape[0] // blocks
+    copies = []
+    for i in range(blocks):
+        own = slice(i * step, (i + 1) * step)
+        chosen = chosen_ref[own, :]
+        feat[own, :] = dot(chosen, high) + dot(chosen, low)
+        span = pl.ds(i * step, step)
+        copies.append(pltpu.make_async_copy(feat.at[span], feat_hbm.at[span], sems.at[i]))
+        copies[-1].start()
+    parts = from_code(got_ref[:, :body, :]) * jnp.exp2(meta[:, 0:1, :])
+    total = jnp.sum(parts, axis=0) * (dec_scale / CODE_TOP)
+    for j in range(body // share):
+        dec[:, j * lanes : (j + 1) * lanes] = total[j * share : (j + 1) * share, :]
+    copies.append(pltpu.make_async_copy(dec, dec_hbm, sems.at[blocks]))
+    copies[-1].start()
+    sums = (meta[:, 3:4, :] + meta[:, 4:5, :] * (1.0 / LOSS_TOP)) * jnp.exp2(meta[:, 2:3, :])
+    loss[...] = jnp.sum(sums, axis=0) * (loss_scale / LOSS_TOP)
+    copies.append(pltpu.make_async_copy(loss, loss_hbm, sems.at[blocks + 1]))
+    copies[-1].start()
+    for copy in copies:
+        copy.wait()
 
 
 def local(
@@ -422,7 +448,13 @@
             shape((1, lanes), f32),
         ),
         in_specs=[VMEM, VMEM],
-        out_specs=(VMEM,) * 3,
+        out_specs=(HBM,) * 3,
+        scratch_shapes=[
+            pltpu.VMEM((owned, channels), f32),
+            pltpu.VMEM((share, width), f32),
+            pltpu.VMEM((1, lanes), f32),
+            pltpu.SemaphoreType.DMA((6,)),
+        ],
         compiler_params=params(32),
         name="finish",
     )(chosen, returned)

time: 32.7 us -> 32.6 us (level)
  no operation moved by 1% of the time
where the time goes in v6:
time: 32.6 us; the launch traced here: 32.3 us
  blocking collectives  11.4 us (35%)
  Pallas kernels  10.4 us (32%)
  starting transfers between devices  7.47 us (23%)
  waiting for transfers between devices  2.2 us (7%)
  between operations  0.78 us (2%)
    all_to_all x1, blocking collectives, local(): lax.all_to_all(joined, 'wide', split_axis=0, concat_axis=0, axis_index_gr...  11.4 us
    all_to_all x1, starting transfers between devices, local(): lax.all_to_all(outgoing.reshape(peers, per_owner, channels), 'wide', spli...  7.4 us
    pallas_call x1, Pallas kernels, local(): pl.pallas_call(gram_kernel, out_shape=(shape((rows, rows), bf16), shape((...  5.97 us
    pallas_call x1, Pallas kernels, local(): pl.pallas_call(pick_kernel, out_shape=shape((rows, channels), bf16), in_s...  2 us
    ppermute x1, waiting for transfers between devices, local(): got = lax.ppermute(send, 'wide', [(i, i ^ 1) for i in range(peers)])  1.33 us
    pallas_call x1, Pallas kernels, local(): pl.pallas_call(functools.partial(finish_kernel, body, per_owner, 1.0 / ma...  1.16 us
    all_to_all x1, waiting for transfers between devices, local(): lax.all_to_all(outgoing.reshape(peers, per_owner, channels), 'wide', spli...  0.86 us
    pallas_call x1, Pallas kernels, local(): pl.pallas_call(gradient_kernel, out_shape=(half_shape, half_shape), in_sp...  0.85 us
  transfers between devices with their start and end apart: 2, of which 2 were waited for; matrix products, arithmetic and copies ran while one was open for 0% of the time, Pallas kernels for 19%

profile of v6, /device:TPU:0, one launch (start us, length us, event | category | flops | bytes accessed | tf_op | source)
XLA Modules:
  0.0 32.3 jit_solution(13610351288668434373)
XLA Ops:
  0.6 0.0 copy-start.1
  0.6 0.0 copy-start.5
  0.7 0.0 copy-start
  0.7 0.0 copy-start.3
  0.7 0.0 copy-start.2
  0.7 2.0 %pick.1 = bf16[256,128]{1,0:T(8,128)(2,1)} custom-call(s32[16,1,16]{2,1,0:T(1,128)} %request_ref.1, bf16[1024,128]{1,0:T(8,128)(2,1)} %feature_hbm.1), custom_call_target="tpu_custom_call" | custom-call | flops 20000000000 | bytes 40000000 | tf_op jit(solution)/shard_map/pick/pallas_call | solution.py:346
  2.7 0.0 copy-start.4
  2.7 7.4 %all-to-all-start = ((bf16[16,16,128]{2,1,0:T(8,128)(2,1)}), bf16[16,16,128]{2,1,0:T(8,128)(2,1)S(1)}, u32[]{:S(2)}, u32[]{:S(2)}) async-start(bf16[16,16,128]{2,1,0:T(8,128)(2,1)} %bitcast.1), calls=%async_computation | async-start | bytes 131072 | tf_op jit(solution)/shard_map/all_to_all | solution.py:362
  10.1 0.0 copy-done.1
  10.1 0.0 copy-done.5
  10.1 0.0 copy-done
  10.1 0.0 copy-done.3
  10.1 0.0 copy-done.2
  10.2 6.0 %gram.1 = (bf16[256,256]{1,0:T(8,128)(2,1)S(1)}, bf16[256,256]{1,0:T(8,128)(2,1)S(1)}, bf16[256,1024]{1,0:T(8,128)(2,1)S(1)}, bf16[256,1024]{1,0:T(8,128)(2,1)S(...) custom-call(s32[1,16]{1,0:T(1,128)S(1)} %copy-done.5, ...), custom_call_target="tpu_custom_call" | custom-call | flops 1879048192 | bytes 9437184 | tf_op jit(solution)/shard_map/gram/pallas_call | solution.py:365
  16.1 0.9 %all-to-all-done = bf16[16,16,128]{2,1,0:T(8,128)(2,1)S(1)} async-done(((bf16[16,16,128]{2,1,0:T(8,128)(2,1)}), bf16[16,16,128]{2,1,0:T(8,128)(2,1)S(1)}, u32[]{:S(2)}, u32[]{:S(2)}) %all-to-all-start) | async-done | bytes 65568 | tf_op jit(solution)/shard_map/all_to_all | solution.py:362
  17.0 0.9 %gradient.1 = (f32[8,88,128]{2,1,0:T(8,128)S(1)}, f32[8,88,128]{2,1,0:T(8,128)S(1)}) custom-call(s32[1]{0:T(128)} %bitcast.parity_ref, bf16[256,128]{1,0:T(8,128)(2,1)S(1)} %bitcast.5, bf16[256,256]{1,0:T(8,128)(2,1)S(1)} %get-tuple-element.16.gram_high_ref, bf16[256,256]{1,0:T(8,128)(2,1)S(1)} %get-tuple-element.17.gram_low_ref, ...), custom_call_target="tpu_custom_call" | custom-call | tf_op jit(solution)/shard_map/gradient/pallas_call | solution.py:399
  17.9 0.1 collective-permute-start
  17.9 0.0 copy-done.4
  18.0 0.3 place.1.after_ref.chosen_ref
  18.3 1.3 %collective-permute-done.got_ref = f32[8,88,128]{2,1,0:T(8,128)S(1)} collective-permute-done((f32[8,88,128]{2,1,0:T(8,128)S(1)}, f32[8,88,128]{2,1,0:T(8,128)S(1)}, u32[]{:S(2)}, u32[]{:S(2)}) %collective-permute-start) | collective-permute-done | bytes 360480 | tf_op jit(solution)/shard_map/ppermute | solution.py:408
  19.6 0.1 join.1
  19.7 11.4 %all_to_all.10.got_ref = s16[8,112,128]{2,1,0:T(8,128)(2,1)S(1)} all-to-all(s16[8,112,128]{2,1,0:T(8,128)(2,1)S(1)} %join.1), channel_id=1, replica_groups={{12,14,8,10,4,6,0,2},{13,15,9,11,5,7,1,3},{28,30,24,26,20,22,16,18},{29..., dimensions={0} | all-to-all | bytes 458752 | tf_op jit(solution)/shard_map/all_to_all | solution.py:428
  31.2 1.2 %finish.1 = (f32[1024,128]{1,0:T(8,128)}, f32[8,1024]{1,0:T(8,128)}, f32[1,128]{1,0:T(1,128)}) custom-call(bf16[1024,256]{1,0:T(8,128)(2,1)S(1)} %place.1.after_ref.chosen_ref, s16[8,112,128]{2,1,0:T(8,128)(2,1)S(1)} %all_to_all.10.got_ref), custom_call_target="tpu_custom_call" | custom-call | tf_op jit(solution)/shard_map/finish/pallas_call | solution.py:437
Async XLA Ops:
  0.6 9.5 %copy-start.1 = (bf16[128,1024]{1,0:T(8,128)(2,1)S(1)}, bf16[128,1024]{1,0:T(8,128)(2,1)}, u32[]{:S(2)}) copy-start(bf16[128,1024]{1,0:T(8,128)(2,1)} %weight_ref.3) | copy-start | bytes 786436
  0.6 9.5 %copy-start.5 = (s32[1,16]{1,0:T(1,128)S(1)}, s32[1,16]{1,0:T(1,128)}, u32[]{:S(2)}) copy-start(s32[1,16]{1,0:T(1,128)} %count_ref.1) | copy-start | bytes 196
  0.7 9.5 %copy-start = (s32[16,64,256]{2,1,0:T(8,128)S(1)}, s32[16,64,256]{2,1,0:T(8,128)}, u32[]{:S(2)}) copy-start(s32[16,64,256]{2,1,0:T(8,128)} %code_ref.1) | copy-start | bytes 3145732
  0.7 9.5 %copy-start.3 = (s32[16,64]{1,0:T(8,128)S(1)}, s32[16,64]{1,0:T(8,128)}, u32[]{:S(2)}) copy-start(s32[16,64]{1,0:T(8,128)} %order_ref.1) | copy-start | bytes 12292
  0.7 9.5 %copy-start.2 = (s32[16,64]{1,0:T(8,128)S(1)}, s32[16,64]{1,0:T(8,128)}, u32[]{:S(2)}) copy-start(s32[16,64]{1,0:T(8,128)} %list_ref.1) | copy-start | bytes 12292
  2.7 15.3 %copy-start.4 = (s32[16,1,16]{2,1,0:T(1,128)S(1)}, s32[16,1,16]{2,1,0:T(1,128)}, u32[]{:S(2)}) copy-start(s32[16,1,16]{2,1,0:T(1,128)} %request_ref.1) | copy-start | bytes 3076
  2.7 14.3 %all-to-all-start = ((bf16[16,16,128]{2,1,0:T(8,128)(2,1)}), bf16[16,16,128]{2,1,0:T(8,128)(2,1)S(1)}, u32[]{:S(2)}, u32[]{:S(2)}) async-start(bf16[16,16,128]{2,1,0:T(8,128)(2,1)} %bitcast.1), calls=%async_computation | async-start | bytes 131072 | tf_op jit(solution)/shard_map/all_to_all | solution.py:362
  17.9 1.7 %collective-permute-start = (f32[8,88,128]{2,1,0:T(8,128)S(1)}, f32[8,88,128]{2,1,0:T(8,128)S(1)}, u32[]{:S(2)}, u32[]{:S(2)}) collective-permute-start(f32[8,88,128]{2,1,0:T(8,128)S(1)} %get-tuple-element.24.after_ref), channel_id=1, source_target_pairs={{0,1},{1,0},{2,3},{3,2},{4,5},{5,4},{6,7},{7,6},{8,9},{9,8},{10,11... | collective-permute-start | bytes 1081352 | tf_op jit(solution)/shard_map/ppermute | solution.py:408

commit v7 on v6

--- a/solution.py
+++ b/solution.py
@@ -50,7 +50,7 @@
     return pltpu.CompilerParams(vmem_limit_bytes=mib << 20)
 
 
-def pick_kernel(request_hbm, feature_hbm, out_ref, wanted, held, sems):
+def pick_kernel(request_hbm, feature_hbm, out_hbm, wanted, held, picked, sems):
     copies = [
         pltpu.make_async_copy(request_hbm, wanted, sems.at[0]),
         pltpu.make_async_copy(feature_hbm, held, sems.at[1]),
@@ -64,7 +64,17 @@
     chosen = jnp.where(wanted[...][:, 0, :][:, :, None] == lane, 1.0, 0.0)
     chosen = chosen.reshape(peers * per_owner, owned).astype(jnp.bfloat16)
     copies[1].wait()
-    out_ref[...] = dot(chosen, held[...]).astype(jnp.bfloat16)
+    half = picked.shape[0] // 2
+    for i in range(2):
+        own = slice(i * half, (i + 1) * half)
+        picked[own, :] = dot(chosen[own], held[...]).astype(jnp.bfloat16)
+        span = pl.ds(i * half, half)
+        copies.append(
+            pltpu.make_async_copy(picked.at[span], out_hbm.at[span], sems.at[2 + i])
+        )
+        copies[-1].start()
+    for copy in copies[2:]:
+        copy.wait()
 
 
 def gram_kernel(
@@ -347,11 +357,12 @@
         pick_kernel,
         out_shape=shape((rows, channels), bf16),
         in_specs=[HBM, HBM],
-        out_specs=VMEM,
+        out_specs=HBM,
         scratch_shapes=[
             pltpu.VMEM((peers, 1, per_owner), jnp.int32),
             pltpu.VMEM((owned, channels), bf16),
-            pltpu.SemaphoreType.DMA((2,)),
+            pltpu.VMEM((rows, channels), bf16),
+            pltpu.SemaphoreType.DMA((4,)),
         ],
         cost_estimate=pl.CostEstimate(
             flops=20_000_000_000, bytes_accessed=40_000_000, transcendentals=0

time: 32.6 us -> 32.6 us (level)
  no operation moved by 1% of the time
where the time goes in v7:
time: 32.6 us; the launch traced here: 32.3 us
  blocking collectives  11.4 us (35%)
  Pallas kernels  10.4 us (32%)
  starting transfers between devices  7.47 us (23%)
  waiting for transfers between devices  2.2 us (7%)
  between operations  0.78 us (2%)
    all_to_all x1, blocking collectives, local(): lax.all_to_all(joined, 'wide', split_axis=0, concat_axis=0, axis_index_gr...  11.4 us
    all_to_all x1, starting transfers between devices, local(): lax.all_to_all(outgoing.reshape(peers, per_owner, channels), 'wide', spli...  7.4 us
    pallas_call x1, Pallas kernels, local(): pl.pallas_call(gram_kernel, out_shape=(shape((rows, rows), bf16), shape((...  5.96 us
    pallas_call x1, Pallas kernels, local(): pl.pallas_call(pick_kernel, out_shape=shape((rows, channels), bf16), in_s...  2 us
    ppermute x1, waiting for transfers between devices, local(): got = lax.ppermute(send, 'wide', [(i, i ^ 1) for i in range(peers)])  1.33 us
    pallas_call x1, Pallas kernels, local(): pl.pallas_call(functools.partial(finish_kernel, body, per_owner, 1.0 / ma...  1.16 us
    all_to_all x1, waiting for transfers between devices, local(): lax.all_to_all(outgoing.reshape(peers, per_owner, channels), 'wide', spli...  0.87 us
    pallas_call x1, Pallas kernels, local(): pl.pallas_call(gradient_kernel, out_shape=(half_shape, half_shape), in_sp...  0.86 us
  transfers between devices with their start and end apart: 2, of which 2 were waited for; matrix products, arithmetic and copies ran while one was open for 0% of the time, Pallas kernels for 19%

profile of v7, /device:TPU:0, one launch (start us, length us, event | category | flops | bytes accessed | tf_op | source)
XLA Modules:
  0.0 32.3 jit_solution(8328314855558246534)
XLA Ops:
  0.6 0.0 copy-start.1
  0.6 0.0 copy-start.5
  0.7 0.0 copy-start
  0.7 0.0 copy-start.3
  0.7 0.0 copy-start.2
  0.7 2.0 %pick.1 = bf16[256,128]{1,0:T(8,128)(2,1)} custom-call(s32[16,1,16]{2,1,0:T(1,128)} %request_ref.1, bf16[1024,128]{1,0:T(8,128)(2,1)} %feature_hbm.1), custom_call_target="tpu_custom_call" | custom-call | flops 20000000000 | bytes 40000000 | tf_op jit(solution)/shard_map/pick/pallas_call | solution.py:356
  2.7 0.0 copy-start.4
  2.7 7.4 %all-to-all-start = ((bf16[16,16,128]{2,1,0:T(8,128)(2,1)}), bf16[16,16,128]{2,1,0:T(8,128)(2,1)S(1)}, u32[]{:S(2)}, u32[]{:S(2)}) async-start(bf16[16,16,128]{2,1,0:T(8,128)(2,1)} %bitcast.1), calls=%async_computation | async-start | bytes 131072 | tf_op jit(solution)/shard_map/all_to_all | solution.py:373
  10.1 0.0 copy-done.1
  10.1 0.0 copy-done.5
  10.1 0.0 copy-done
  10.1 0.0 copy-done.3
  10.2 0.0 copy-done.2
  10.2 6.0 %gram.1 = (bf16[256,256]{1,0:T(8,128)(2,1)S(1)}, bf16[256,256]{1,0:T(8,128)(2,1)S(1)}, bf16[256,1024]{1,0:T(8,128)(2,1)S(1)}, bf16[256,1024]{1,0:T(8,128)(2,1)S(...) custom-call(s32[1,16]{1,0:T(1,128)S(1)} %copy-done.5, ...), custom_call_target="tpu_custom_call" | custom-call | flops 1879048192 | bytes 9437184 | tf_op jit(solution)/shard_map/gram/pallas_call | solution.py:376
  16.1 0.9 %all-to-all-done = bf16[16,16,128]{2,1,0:T(8,128)(2,1)S(1)} async-done(((bf16[16,16,128]{2,1,0:T(8,128)(2,1)}), bf16[16,16,128]{2,1,0:T(8,128)(2,1)S(1)}, u32[]{:S(2)}, u32[]{:S(2)}) %all-to-all-start) | async-done | bytes 65568 | tf_op jit(solution)/shard_map/all_to_all | solution.py:373
  17.0 0.9 %gradient.1 = (f32[8,88,128]{2,1,0:T(8,128)S(1)}, f32[8,88,128]{2,1,0:T(8,128)S(1)}) custom-call(s32[1]{0:T(128)} %bitcast.parity_ref, bf16[256,128]{1,0:T(8,128)(2,1)S(1)} %bitcast.5, bf16[256,256]{1,0:T(8,128)(2,1)S(1)} %get-tuple-element.16.gram_high_ref, bf16[256,256]{1,0:T(8,128)(2,1)S(1)} %get-tuple-element.17.gram_low_ref, ...), custom_call_target="tpu_custom_call" | custom-call | tf_op jit(solution)/shard_map/gradient/pallas_call | solution.py:410
  17.9 0.1 collective-permute-start
  17.9 0.0 copy-done.4
  18.0 0.3 place.1.after_ref.chosen_ref
  18.3 1.3 %collective-permute-done.got_ref = f32[8,88,128]{2,1,0:T(8,128)S(1)} collective-permute-done((f32[8,88,128]{2,1,0:T(8,128)S(1)}, f32[8,88,128]{2,1,0:T(8,128)S(1)}, u32[]{:S(2)}, u32[]{:S(2)}) %collective-permute-start) | collective-permute-done | bytes 360480 | tf_op jit(solution)/shard_map/ppermute | solution.py:419
  19.6 0.1 join.1
  19.7 11.4 %all_to_all.10.got_ref = s16[8,112,128]{2,1,0:T(8,128)(2,1)S(1)} all-to-all(s16[8,112,128]{2,1,0:T(8,128)(2,1)S(1)} %join.1), channel_id=1, replica_groups={{12,14,8,10,4,6,0,2},{13,15,9,11,5,7,1,3},{28,30,24,26,20,22,16,18},{29..., dimensions={0} | all-to-all | bytes 458752 | tf_op jit(solution)/shard_map/all_to_all | solution.py:439
  31.1 1.2 %finish.1 = (f32[1024,128]{1,0:T(8,128)}, f32[8,1024]{1,0:T(8,128)}, f32[1,128]{1,0:T(1,128)}) custom-call(bf16[1024,256]{1,0:T(8,128)(2,1)S(1)} %place.1.after_ref.chosen_ref, s16[8,112,128]{2,1,0:T(8,128)(2,1)S(1)} %all_to_all.10.got_ref), custom_call_target="tpu_custom_call" | custom-call | tf_op jit(solution)/shard_map/finish/pallas_call | solution.py:448
Async XLA Ops:
  0.6 9.5 %copy-start.1 = (bf16[128,1024]{1,0:T(8,128)(2,1)S(1)}, bf16[128,1024]{1,0:T(8,128)(2,1)}, u32[]{:S(2)}) copy-start(bf16[128,1024]{1,0:T(8,128)(2,1)} %weight_ref.3) | copy-start | bytes 786436
  0.6 9.5 %copy-start.5 = (s32[1,16]{1,0:T(1,128)S(1)}, s32[1,16]{1,0:T(1,128)}, u32[]{:S(2)}) copy-start(s32[1,16]{1,0:T(1,128)} %count_ref.1) | copy-start | bytes 196
  0.7 9.5 %copy-start = (s32[16,64,256]{2,1,0:T(8,128)S(1)}, s32[16,64,256]{2,1,0:T(8,128)}, u32[]{:S(2)}) copy-start(s32[16,64,256]{2,1,0:T(8,128)} %code_ref.1) | copy-start | bytes 3145732
  0.7 9.5 %copy-start.3 = (s32[16,64]{1,0:T(8,128)S(1)}, s32[16,64]{1,0:T(8,128)}, u32[]{:S(2)}) copy-start(s32[16,64]{1,0:T(8,128)} %order_ref.1) | copy-start | bytes 12292
  0.7 9.5 %copy-start.2 = (s32[16,64]{1,0:T(8,128)S(1)}, s32[16,64]{1,0:T(8,128)}, u32[]{:S(2)}) copy-start(s32[16,64]{1,0:T(8,128)} %list_ref.1) | copy-start | bytes 12292
  2.7 15.3 %copy-start.4 = (s32[16,1,16]{2,1,0:T(1,128)S(1)}, s32[16,1,16]{2,1,0:T(1,128)}, u32[]{:S(2)}) copy-start(s32[16,1,16]{2,1,0:T(1,128)} %request_ref.1) | copy-start | bytes 3076
  2.7 14.3 %all-to-all-start = ((bf16[16,16,128]{2,1,0:T(8,128)(2,1)}), bf16[16,16,128]{2,1,0:T(8,128)(2,1)S(1)}, u32[]{:S(2)}, u32[]{:S(2)}) async-start(bf16[16,16,128]{2,1,0:T(8,128)(2,1)} %bitcast.1), calls=%async_computation | async-start | bytes 131072 | tf_op jit(solution)/shard_map/all_to_all | solution.py:373
  17.9 1.7 %collective-permute-start = (f32[8,88,128]{2,1,0:T(8,128)S(1)}, f32[8,88,128]{2,1,0:T(8,128)S(1)}, u32[]{:S(2)}, u32[]{:S(2)}) collective-permute-start(f32[8,88,128]{2,1,0:T(8,128)S(1)} %get-tuple-element.24.after_ref), channel_id=1, source_target_pairs={{0,1},{1,0},{2,3},{3,2},{4,5},{5,4},{6,7},{7,6},{8,9},{9,8},{10,11... | collective-permute-start | bytes 1081352 | tf_op jit(solution)/shard_map/ppermute | solution.py:419
